TPU v7x, 32 devices: a whole 2x2x4 slice. The times are simulated.
32 devices in a mesh: dp: 8 (over y, x, core), seq: 4 (over z).
Axes of the slice: x: 2, y: 2, z: 4, core: 2. Of those that a mesh axis runs over, the one named last changes fastest.
Arguments:
- inputs: bfloat16 [16, 2048, 1024], P('dp', 'seq'), may hold values from -8 to 8
- w_qkv: bfloat16 [1024, 3072], replicated, may hold values from -0.1875 to 0.1875
- w_out: bfloat16 [1024, 1024], replicated, may hold values from -0.75 to 0.75
- w_gate_up: bfloat16 [1024, 5504], replicated, may hold values from -0.1875 to 0.1875
- w_down: bfloat16 [1024, 2752], replicated, may hold values from -0.15625 to 0.15625
- gain_attn: float32 [1024], replicated, may hold values from 0.5 to 1.5
- gain_mlp: float32 [1024], replicated, may hold values from 0.5 to 1.5
- doc_start: int32 [16, 2048], P('dp', 'seq'), may hold values from 0 to 2047, as said below
- cotangent: bfloat16 [16, 2048, 1024], P('dp', 'seq'), may hold values from -8 to 8
Outputs:
- outputs: bfloat16 [16, 2048, 1024], P('dp', 'seq')
- grad_inputs: float32 [16, 2048, 1024], P('dp', 'seq')
- grad_qkv: float32 [1024, 3072], P('seq')
- grad_out: float32 [1024, 1024], P('seq')
- grad_gate_up: float32 [1024, 5504], P('seq')
- grad_down: float32 [1024, 2752], P('seq')
- grad_gain_attn: float32 [1024], P('seq')
- grad_gain_mlp: float32 [1024], P('seq')
Inputs may be any that keep to these rules, and one draw needn't show every extreme that they name: doc_start[r, 0] = 0, and doc_start[r, i] is either i or doc_start[r, i - 1]. Of the 2 rows of each index of dp, one holds a single document from some position below 512 to the row's end.
All inputs are finite; a program needn't handle non-finite values.
Results may differ from a plain program's by a relative error of at most 0.019.
Values may be sent and summed in bfloat16 or wider, within the bound.
No kernel may reach another device: no remote copies, remote signals or barrier semaphores. Data moves between devices by JAX's collectives and lax.ppermute only.
A program may use at most 320 MiB of HBM per device.

v0:
```python
import functools
import math

import jax
import jax.numpy as jnp
import numpy as np
from jax import lax
from jax.experimental import pallas as pl
from jax.experimental.pallas import tpu as pltpu
from jax.sharding import PartitionSpec as P

HEADS = 16
HEAD_DIM = 64
FF = 2752
WINDOW = 64
LANES = 128
PAIRS = 2
FF_TILE = 256
FF_TILES = -(-FF // FF_TILE)
FF_CHUNKS = (6, 5)
STEP = 256
epsilon = 1e-05
masked_value = -1e30
F32 = jnp.float32
BF16 = jnp.bfloat16
VMEM_LIMIT = 64 * 1024 * 1024 - 256 * 1024
PER_US = 1.1e9


def dot(left, right, left_dim=1, right_dim=0):
    return lax.dot_general(
        left, right, (((left_dim,), (right_dim,)), ((), ())), preferred_element_type=F32
    )


def launch(kernel, name, grid, scalars, inputs, outputs, scratch=(), us=8, after=()):
    known = len(scalars) + len(inputs)

    def body(*refs):
        kernel(*refs[:known], *refs[known + len(after) :])

    specs = [spec for _, spec in inputs] + [pl.BlockSpec(memory_space=pl.ANY)] * len(after)
    shapes = [pltpu.HBM(shape, kind) for shape, kind, _ in outputs]
    moved = sum(array.size * array.dtype.itemsize for array, _ in inputs)
    moved += sum(math.prod(shape) * np.dtype(kind).itemsize for shape, kind, _ in outputs)
    return pl.pallas_call(
        body,
        grid_spec=pltpu.PrefetchScalarGridSpec(
            num_scalar_prefetch=len(scalars),
            grid=grid,
            in_specs=specs,
            out_specs=[spec for _, _, spec in outputs],
            scratch_shapes=list(scratch),
        ),
        out_shape=shapes,
        compiler_params=pltpu.CompilerParams(vmem_limit_bytes=VMEM_LIMIT),
        cost_estimate=pl.CostEstimate(flops=int(us * PER_US), bytes_accessed=int(moved / 100), transcendentals=0),
        name=name,
    )(*scalars, *[array for array, _ in inputs], *after)


def full(*shape):
    return pl.BlockSpec(shape, lambda *_: (0,) * len(shape))


CORE_INDEX, SEQ_INDEX, POSITION = range(3)


def store_slabs(out_ref, value, facts_ref, first, slab, columns=slice(None)):
    for k in range(value.shape[0] // slab):
        row = pl.multiple_of(facts_ref[first + k] * slab, slab)
        out_ref[pl.ds(row, slab), columns] = value[k * slab : (k + 1) * slab]


def side_by_side(ref):
    return jnp.concatenate([ref[k] for k in range(ref.shape[0])], axis=1)


def put_blocks(ref, value, rows=slice(None)):
    for k in range(ref.shape[0]):
        ref[k, rows, :] = value[:, k * LANES : (k + 1) * LANES]

def two_heads(value, low):
    zero = jnp.zeros_like(value)
    return jnp.concatenate([jnp.where(low, value, zero), jnp.where(low, zero, value)], axis=0)


def one_of_two(value, size):
    feature = lax.broadcasted_iota(jnp.int32, (LANES, size), 0)
    return jnp.where(feature < HEAD_DIM, value[:, :size], value[:, size:])


class Spans:
    def __init__(self, rows, group):
        self.rows, self.group = rows, group
        self.size = min(128, group)
        self.blocks = group // self.size
        self.count = rows * self.blocks
        self.window = self.size + WINDOW

    def queries(self, at):
        return slice(at * self.size, (at + 1) * self.size)

    def keys(self, own_ref, rim_ref, pair, at):
        row, block = divmod(at, self.blocks)
        start = at * self.size
        if block == 0:
            rim = rim_ref[pair, row * WINDOW : (row + 1) * WINDOW, :]
            return jnp.concatenate([rim, own_ref[pair, start : start + self.size, :]], axis=0)
        return own_ref[pair, start - WINDOW : start + self.size, :]

    def fill_bias(self, bias_ref, starts_ref, facts_ref):
        size = self.size
        key = lax.broadcasted_iota(jnp.int32, (self.window, size), 0) - WINDOW
        query = lax.broadcasted_iota(jnp.int32, (self.window, size), 1)
        near = (key <= query) & (query - key <= WINDOW)
        for at in range(self.count):
            row, block = divmod(at, self.blocks)
            begin = starts_ref[row : row + 1, block * size : (block + 1) * size]
            begin = begin - facts_ref[POSITION] - block * size
            bias = jnp.where(near & (key >= begin), 0.0, masked_value).astype(F32)
            bias_ref[at, :, :size] = bias
            bias_ref[at, :, size:] = bias

    def scratch(self, kind):
        return pltpu.VMEM((self.count, self.window, 2 * self.size), kind)


def softmax(scores):
    weights = jnp.exp(scores - jnp.max(scores, axis=0, keepdims=True))
    return weights * (1.0 / jnp.sum(weights, axis=0, keepdims=True))


def attend_kernel(facts_ref, starts_ref, q_ref, k_ref, v_ref, kr_ref, vr_ref,
                  att_ref, attT_ref, bias_ref, score_ref, probs_ref, *, spans, slab, put, pairs):
    step = pl.program_id(0)
    size, count = spans.size, spans.count

    @pl.when(step == 0)
    def _():
        spans.fill_bias(bias_ref, starts_ref, facts_ref)

    low = lax.broadcasted_iota(jnp.int32, (size, LANES), 1) < HEAD_DIM
    for pair in range(pairs):
        for at in range(count):
            queries = q_ref[pair, spans.queries(at), :] * jnp.asarray(HEAD_DIM ** (-0.5), BF16)
            keys = spans.keys(k_ref, kr_ref, pair, at)
            score_ref[at] = dot(keys, two_heads(queries, low), 1, 1)
        for at in range(count):
            probs_ref[at] = softmax(score_ref[at] + bias_ref[at]).astype(BF16)
        for at in range(count):
            values = spans.keys(v_ref, vr_ref, pair, at)
            mixed = one_of_two(dot(values, probs_ref[at], 0, 0), size)
            att_ref[pair, spans.queries(at), :] = mixed.T.astype(BF16)
            first = put + (step * pairs + pair) * (LANES // slab)
            store_slabs(attT_ref, mixed.astype(BF16), facts_ref, first, slab, spans.queries(at))


def attend(qkv, kv_rim, doc_start, facts, put, slab, after=()):
    rows, group = doc_start.shape
    all_pairs, tokens = qkv.shape[0] // 3, qkv.shape[1]
    rim = kv_rim.shape[1]
    spans = Spans(rows, group)
    steps = all_pairs // PAIRS
    own = lambda kind: pl.BlockSpec((PAIRS, tokens, LANES), lambda j, *_: (kind * steps + j, 0, 0))
    edge = lambda kind: pl.BlockSpec((PAIRS, rim, LANES), lambda j, *_: (kind * steps + j, 0, 0))
    width = all_pairs * LANES
    return launch(
        functools.partial(attend_kernel, spans=spans, slab=slab, put=put, pairs=PAIRS),
        "attend",
        (steps,),
        [facts],
        [
            (doc_start, full(rows, group)),
            (qkv, own(0)),
            (qkv, own(1)),
            (qkv, own(2)),
            (kv_rim, edge(0)),
            (kv_rim, edge(1)),
        ],
        [
            ((all_pairs, tokens, LANES), BF16, own(0)),
            ((width, tokens), BF16, full(width, tokens)),
        ],
        [spans.scratch(F32), spans.scratch(F32), spans.scratch(BF16)],
        us=8,
        after=after,
    )


def attend_back_kernel(facts_ref, starts_ref, q_ref, k_ref, v_ref, kr_ref, vr_ref, da_ref,
                       dqkv_ref, drim_ref,
                       bias_ref, score_ref, grad_ref, probs_ref, dscore_ref, *, spans, pairs):
    size, count = spans.size, spans.count

    @pl.when(pl.program_id(0) == 0)
    def _():
        spans.fill_bias(bias_ref, starts_ref, facts_ref)

    low = lax.broadcasted_iota(jnp.int32, (size, LANES), 1) < HEAD_DIM
    scale = HEAD_DIM ** (-0.5)

    def scaled_queries(pair, at):
        return two_heads(q_ref[pair, spans.queries(at), :] * jnp.asarray(scale, BF16), low)

    for pair in range(pairs):
        for at in range(count):
            score_ref[at] = dot(spans.keys(k_ref, kr_ref, pair, at), scaled_queries(pair, at), 1, 1)
            grads = two_heads(da_ref[pair, spans.queries(at), :], low)
            grad_ref[at] = dot(spans.keys(v_ref, vr_ref, pair, at), grads, 1, 1)
        for at in range(count):
            probs = softmax(score_ref[at] + bias_ref[at])
            probs_ref[at] = probs.astype(BF16)
            part = probs * grad_ref[at]
            dscore_ref[at] = (part - probs * jnp.sum(part, axis=0, keepdims=True)).astype(BF16)
        late = [None, None]
        for at in range(count):
            here = spans.queries(at)
            row, block = divmod(at, spans.blocks)
            dscores = dscore_ref[at]
            grads = two_heads(da_ref[pair, here, :], low)
            dk = dot(dscores, scaled_queries(pair, at))
            dv = dot(probs_ref[at], grads)
            dq = one_of_two(dot(spans.keys(k_ref, kr_ref, pair, at), dscores, 0, 0), size) * scale
            dqkv_ref[0, pair, here, :] = dq.T.astype(BF16)
            start = at * size
            for kind, grad in ((0, dk), (1, dv)):
                out_ref, rim_ref = dqkv_ref.at[kind + 1], drim_ref.at[kind]
                early = grad[:WINDOW]
                if block == 0:
                    rim_ref[pair, row * WINDOW : (row + 1) * WINDOW, :] = early.astype(BF16)
                else:
                    out_ref[pair, start - WINDOW : start, :] = (late[kind] + early).astype(BF16)
                if size > WINDOW:
                    out_ref[pair, start : start + size - WINDOW, :] = grad[WINDOW:size].astype(BF16)
                late[kind] = grad[size:]
                if block == spans.blocks - 1:
                    out_ref[pair, start + size - WINDOW : start + size, :] = late[kind].astype(BF16)


def attend_back(qkv, kv_rim, doc_start, facts, grad_att, after=()):
    rows, group = doc_start.shape
    all_pairs, tokens = qkv.shape[0] // 3, qkv.shape[1]
    rim = kv_rim.shape[1]
    spans = Spans(rows, group)
    steps = all_pairs // PAIRS
    own = lambda kind: pl.BlockSpec((PAIRS, tokens, LANES), lambda j, *_: (kind * steps + j, 0, 0))
    edge = lambda kind: pl.BlockSpec((PAIRS, rim, LANES), lambda j, *_: (kind * steps + j, 0, 0))
    return launch(
        functools.partial(attend_back_kernel, spans=spans, pairs=PAIRS),
        "attend_back",
        (steps,),
        [facts],
        [
            (doc_start, full(rows, group)),
            (qkv, own(0)),
            (qkv, own(1)),
            (qkv, own(2)),
            (kv_rim, edge(0)),
            (kv_rim, edge(1)),
            (grad_att, own(0)),
        ],
        [
            ((3, all_pairs, tokens, LANES), BF16, pl.BlockSpec((3, PAIRS, tokens, LANES), lambda j, *_: (0, j, 0, 0))),
            ((2, all_pairs, rim, LANES), BF16, pl.BlockSpec((2, PAIRS, rim, LANES), lambda j, *_: (0, j, 0, 0))),
        ],
        [spans.scratch(kind) for kind in (F32, F32, F32, BF16, BF16)],
        us=8,
        after=after,
    )


def norm_matmul_kernel(facts_ref, x_ref, gain_ref, w_ref, out_ref, normedT_ref, tail_ref, normed_ref, *, slab, put, step, tails):
    @pl.when(pl.program_id(0) == 0)
    def _():
        for at in range(0, x_ref.shape[0], step):
            x = x_ref[at : at + step, :].astype(F32)
            inv = lax.rsqrt(jnp.mean(x * x, axis=-1, keepdims=True) + epsilon)
            normed = (x * inv * gain_ref[...]).astype(BF16)
            normed_ref[at : at + step, :] = normed
            store_slabs(normedT_ref, normed.T, facts_ref, put, slab, slice(at, at + step))

        for k, end in enumerate(tails):
            tail_ref[k * WINDOW : (k + 1) * WINDOW, :] = x_ref[end - WINDOW : end, :]

    put_blocks(out_ref, dot(normed_ref[...], w_ref[...]).astype(BF16))


def norm_matmul(x, gain, weight, first_column, facts, put, slab, tails, after=()):
    tokens, width = x.shape
    columns = weight.shape[1] - first_column
    tile = 1024
    skip, wide = first_column // tile, tile // LANES
    return launch(
        functools.partial(norm_matmul_kernel, slab=slab, put=put, step=min(STEP, tokens), tails=tails),
        "norm_matmul",
        (columns // tile,),
        [facts],
        [
            (x, full(tokens, width)),
            (gain[None], full(1, width)),
            (weight, pl.BlockSpec((width, tile), lambda j, *_: (0, skip + j))),
        ],
        [
            ((columns // LANES, tokens, LANES), BF16, pl.BlockSpec((wide, tokens, LANES), lambda j, *_: (j, 0, 0))),
            ((width, tokens), BF16, full(width, tokens)),
            ((len(tails) * WINDOW, width), BF16, full(len(tails) * WINDOW, width)),
        ],
        [pltpu.VMEM((tokens, width), BF16)],
        us=8,
        after=after,
    )


def turn_kernel(facts_ref, x_ref, out_ref, *, slab, put):
    store_slabs(out_ref, x_ref[...].T, facts_ref, put, slab)


def turn(x, facts, put, slab, after=()):
    tokens, width = x.shape
    step = 2 * STEP
    return launch(
        functools.partial(turn_kernel, slab=slab, put=put),
        "turn",
        (tokens // step,),
        [facts],
        [(x, pl.BlockSpec((step, width), lambda m, *_: (m, 0)))],
        [((width, tokens), BF16, pl.BlockSpec((width, step), lambda m, *_: (0, m)))],
        us=8,
        after=after,
    )[0]


def out_proj_kernel(facts_ref, att_ref, w_ref, x_ref, gain_ref, resid_ref, normed_ref, normedT_ref, *, slab, put):
    resid = x_ref[...].astype(F32) + dot(side_by_side(att_ref), w_ref[...])
    resid_ref[...] = resid.astype(BF16)
    inv = lax.rsqrt(jnp.mean(resid * resid, axis=-1, keepdims=True) + epsilon)
    normed = (resid * inv * gain_ref[...]).astype(BF16)
    normed_ref[...] = normed
    store_slabs(normedT_ref, normed.T, facts_ref, put, slab)


def out_proj(att, w_out, x, gain, facts, put, slab, after=()):
    tokens, width = x.shape
    pairs = att.shape[0]
    step = 2 * STEP
    rows = pl.BlockSpec((step, width), lambda m, *_: (m, 0))
    return launch(
        functools.partial(out_proj_kernel, slab=slab, put=put),
        "out_proj",
        (tokens // step,),
        [facts],
        [
            (att, pl.BlockSpec((pairs, step, LANES), lambda m, *_: (0, m, 0))),
            (w_out, full(width, width)),
            (x, rows),
            (gain[None], full(1, width)),
        ],
        [
            ((tokens, width), BF16, rows),
            ((tokens, width), BF16, rows),
            ((width, tokens), BF16, pl.BlockSpec((width, step), lambda m, *_: (0, m))),
        ],
        us=8,
        after=after,
    )


def ff_kernel(*refs, first, given, ends):
    normed_ref, dy_ref, dyT_ref, normedT_ref, wg_ref, wu0_ref, wu1_ref, wu2_ref, wd_ref = refs[:9]
    rest = list(refs[9:])
    total_in = rest.pop(0) if given else None
    if ends:
        resid_ref, gain_ref, w_out_ref = rest[:3]
        rest = rest[3:]
    hidden_ref, dgu_ref, send_down, send_gate, send_up, *totals, acc_ref = rest
    tile = pl.program_id(0)
    tokens = normed_ref.shape[0]

    @pl.when(tile == 0)
    def _():
        acc_ref[...] = total_in[...] if given else jnp.zeros_like(acc_ref)

    half = FF % LANES
    w_both = jnp.concatenate([wg_ref[...], wu0_ref[:, half:], wu1_ref[...], wu2_ref[:, :half]], axis=1)
    limit = FF - (tile + first) * FF_TILE
    inside = lax.broadcasted_iota(jnp.int32, (STEP, FF_TILE), 1) < limit

    def products(at):
        here = slice(at, at + STEP)
        both = dot(normed_ref[here, :], w_both)
        return both[:, :FF_TILE], both[:, FF_TILE:], dot(dy_ref[here, :], wd_ref[...], 1, 1)

    def act(at, gate, up, back):
        here = slice(at, at + STEP)
        sigma = 1.0 / (1.0 + jnp.exp(-gate))
        silu = gate * sigma
        hidden_ref[here, :] = jnp.where(inside, silu * up, 0.0).astype(BF16)
        dgate = back * up * (sigma * (1.0 + gate * (1.0 - sigma)))
        dgu_ref[0, here, :] = jnp.where(inside, dgate, 0.0).astype(BF16)
        dgu_ref[1, here, :] = jnp.where(inside, back * silu, 0.0).astype(BF16)

    def norm_grad(at):
        here = slice(at, at + STEP)
        grads = jnp.concatenate([dgu_ref[0, here, :], dgu_ref[1, here, :]], axis=1)
        acc_ref[here, :] += dot(grads, w_both, 1, 1)

    held = products(0)
    for at in range(0, tokens, STEP):
        ahead = products(at + STEP) if at + STEP < tokens else None
        act(at, *held)
        norm_grad(at)
        held = ahead
    send_down[...] = dot(dyT_ref[...], hidden_ref[...]).astype(BF16)
    both = dot(normedT_ref[...], jnp.concatenate([dgu_ref[0], dgu_ref[1]], axis=1)).astype(BF16)
    send_gate[...] = both[:, :FF_TILE]
    send_up[...] = both[:, FF_TILE:]

    @pl.when(tile == pl.num_programs(0) - 1)
    def _():
        if not ends:
            totals[0][...] = acc_ref[...]
            return
        drb_ref, da_ref = totals
        for at in range(0, tokens, STEP):
            here = slice(at, at + STEP)
            grad = norm_back(acc_ref[here, :], resid_ref[here, :].astype(F32), gain_ref[...])
            branch = (dy_ref[here, :].astype(F32) + grad).astype(BF16)
            put_blocks(drb_ref, branch, here)
            put_blocks(da_ref, dot(branch, w_out_ref[...], 1, 1).astype(BF16), here)


def feed_forward(normed, dy, dy_turned, normed_turned, w_gate_up, w_down, first, count, total=None, end=None, after=()):
    tokens, width = normed.shape
    wide = count * FF_TILE
    last = w_gate_up.shape[1] // LANES - 1
    skip = FF // LANES + first * (FF_TILE // LANES)
    up = lambda k: pl.BlockSpec(
        (width, LANES), lambda j: (0, jnp.minimum(skip + k + j * (FF_TILE // LANES), last))
    )
    other_half = full(width // 2, tokens)
    given = [] if total is None else [(total, full(tokens, width))]
    ending, results = [], [((tokens, width), F32, full(tokens, width))]
    if end is not None:
        resid, gain, w_out = end
        ending = [(resid, full(tokens, width)), (gain[None], full(1, width)), (w_out, full(width, width))]
        blocks = (width // LANES, tokens, LANES)
        results = [(blocks, BF16, full(*blocks))] * 2
    return launch(
        functools.partial(ff_kernel, first=first, given=len(given), ends=end is not None),
        "feed_forward",
        (count,),
        [],
        [
            (normed, full(tokens, width)),
            (dy, full(tokens, width)),
            (dy_turned, other_half),
            (normed_turned, other_half),
            (w_gate_up, pl.BlockSpec((width, FF_TILE), lambda j: (0, first + j))),
            (w_gate_up, up(0)),
            (w_gate_up, up(1)),
            (w_gate_up, up(2)),
            (w_down.T, pl.BlockSpec((FF_TILE, width), lambda j: (first + j, 0))),
        ]
        + given
        + ending,
        [
            ((tokens, wide), BF16, pl.BlockSpec((tokens, FF_TILE), lambda j: (0, j))),
            ((2, tokens, wide), BF16, pl.BlockSpec((2, tokens, FF_TILE), lambda j: (0, 0, j))),
        ]
        + [((width // 2, wide), BF16, pl.BlockSpec((width // 2, FF_TILE), lambda j: (0, j)))] * 3
        + results,
        [pltpu.VMEM((tokens, width), F32)],
        us=8,
        after=after,
    )


def ff_grad_kernel(facts_ref, dyT_ref, normedT_ref, hidden_ref, dgu_ref, got_down, got_gate, got_up, send_ref, keep_ref, *, bit):
    part = send_ref.shape[1]
    own = facts_ref[bit]
    rights = (hidden_ref[...], dgu_ref[0], dgu_ref[1])
    lefts, gots = (dyT_ref, normedT_ref, normedT_ref), (got_down, got_gate, got_up)
    for kind, (left_ref, right, got_ref) in enumerate(zip(lefts, rights, gots)):
        for out_ref, index in ((send_ref, 1 - own), (keep_ref, own)):
            rows = pl.ds(pl.multiple_of(index * part, part), part)
            total = dot(left_ref[rows, :], right) + got_ref[rows, :].astype(F32)
            out_ref[kind] = total.astype(BF16)


def ff_grad(facts, bit, dy_turned, normed_turned, hidden, dgu, got, after=()):
    width, tokens = dy_turned.shape
    wide = hidden.shape[1]
    tile = 512 if wide % 512 == 0 else FF_TILE
    own_half = pl.BlockSpec((width // 2, tokens), lambda j, *_: (1, 0))
    part = ((3, width // 4, wide), BF16, pl.BlockSpec((3, width // 4, tile), lambda j, *_: (0, 0, j)))
    return launch(
        functools.partial(ff_grad_kernel, bit=bit),
        "ff_grad",
        (wide // tile,),
        [facts],
        [
            (dy_turned, own_half),
            (normed_turned, own_half),
            (hidden, pl.BlockSpec((tokens, tile), lambda j, *_: (0, j))),
            (dgu, pl.BlockSpec((2, tokens, tile), lambda j, *_: (0, 0, j))),
        ]
        + [(part, pl.BlockSpec((width // 2, tile), lambda j, *_: (0, j))) for part in got],
        [part, part],
        us=8,
        after=after,
    )


def norm_back(grad, values, gain):
    inv = lax.rsqrt(jnp.mean(values * values, axis=-1, keepdims=True) + epsilon)
    scaled = grad * gain
    return inv * scaled - values * (inv * inv * inv) * jnp.mean(scaled * values, axis=-1, keepdims=True)


def ff_out_kernel(*refs):
    wd_ref, resid_ref, out_ref = refs[-3:]
    total, first = resid_ref[...].astype(F32), 0
    for hidden_ref in refs[:-3]:
        count = min(hidden_ref.shape[1], FF - first)
        total += dot(hidden_ref[:, :count], wd_ref[first : first + count, :])
        first += count
    out_ref[...] = total.astype(BF16)


def ff_out(hiddens, w_down, resid, after=()):
    tokens, width = resid.shape
    rows = lambda columns: pl.BlockSpec((STEP, columns), lambda m: (m, 0))
    return launch(
        ff_out_kernel,
        "ff_out",
        (tokens // STEP,),
        [],
        [(hidden, rows(hidden.shape[1])) for hidden in hiddens]
        + [(w_down.T, full(FF, width)), (resid, rows(width))],
        [((tokens, width), BF16, rows(width))],
        us=1,
        after=after,
    )[0]


def att_grad_kernel(facts_ref, *refs, bit):
    split = bit is not None
    attT_ref, oneT_ref, rimT_ref, drb_ref, dqkv_ref, drim_ref = refs[:6]
    kind = pl.program_id(0)

    def put(total, index):
        if split:
            got_ref = refs[6 + index]
            send_ref, keep_ref = refs[-2:]
            part = send_ref.shape[0]
            own = facts_ref[bit]
            for out_ref, half in ((send_ref, 1 - own), (keep_ref, own)):
                rows = pl.ds(pl.multiple_of(half * part, part), part)
                out_ref[...] = (total(rows) + got_ref[rows, :].astype(F32)).astype(BF16)
        else:
            refs[6 + index][...] = total(slice(None)).astype(BF16)

    @pl.when(kind == 0)
    def _():
        right = side_by_side(drb_ref)
        put(lambda rows: dot(attT_ref[rows, :], right), 0)

    @pl.when(kind == 1)
    def _():
        right = side_by_side(dqkv_ref)
        put(lambda rows: dot(oneT_ref[rows, :], right), 1)

    for index in (2, 3):

        @pl.when(kind == index)
        def _():
            right, rim = side_by_side(dqkv_ref), side_by_side(drim_ref)
            put(lambda rows: dot(oneT_ref[rows, :], right) + dot(rimT_ref[rows, :], rim), index)


def att_grad(facts, att_turned, one_turned, rim_turned, drb, dqkv, drim, bit=None, got=None, us=8, after=()):
    width, tokens = one_turned.shape
    rim = rim_turned.shape[1]
    split = got is not None
    half = 1 if split else 0
    inputs = [
        (turned, pl.BlockSpec((width // 2, turned.shape[1]), lambda j, *_: (half, 0)))
        for turned in (att_turned, one_turned, rim_turned)
    ]
    blocks = width // LANES
    inputs += [
        (drb, full(blocks, tokens, LANES)),
        (dqkv, pl.BlockSpec((None, blocks, tokens, LANES), lambda j, *_: (jnp.maximum(j - 1, 0), 0, 0, 0))),
        (drim, pl.BlockSpec((None, blocks, rim, LANES), lambda j, *_: (jnp.maximum(j - 2, 0), 0, 0, 0))),
    ]
    columns = 4 * width
    parts = [full(width // 2, width)] * 4
    if split:
        inputs += list(zip(got, parts))
        part = ((width // 4, columns), BF16, pl.BlockSpec((width // 4, width), lambda j, *_: (0, j)))
        outputs = [part, part]
    else:
        outputs = [((width // 2, width), BF16, spec) for spec in parts]
    return launch(
        functools.partial(att_grad_kernel, bit=bit),
        "att_grad",
        (4,),
        [facts],
        inputs,
        outputs,
        us=us,
        after=after,
    )


def input_grad_kernel(dqkv_ref, w_ref, x_ref, gain_ref, drb_ref, back_ref, out_ref, acc_ref, *, rows, group):
    k = pl.program_id(0)
    tokens = acc_ref.shape[0]
    part = dot(side_by_side(dqkv_ref), w_ref[...], 1, 1)

    @pl.when(k == 0)
    def _():
        acc_ref[...] = part

    @pl.when(k > 0)
    def _():
        acc_ref[...] += part

    @pl.when(k == 2)
    def _():
        for at in range(0, tokens, STEP):
            here = slice(at, at + STEP)
            grad = norm_back(acc_ref[here, :], x_ref[here, :].astype(F32), gain_ref[...])
            out_ref[here, :] = grad + side_by_side(drb_ref.at[:, here, :]).astype(F32)
        for row in range(rows):
            tail = slice((row + 1) * group - WINDOW, (row + 1) * group)
            out_ref[tail, :] += back_ref[row * WINDOW : (row + 1) * WINDOW, :].astype(F32)


def input_grad(dqkv, w_qkv, x, gain, drb, back, rows, group, after=()):
    tokens, width = x.shape
    whole = full(tokens, width)
    return launch(
        functools.partial(input_grad_kernel, rows=rows, group=group),
        "input_grad",
        (3,),
        [],
        [
            (dqkv, pl.BlockSpec((None, width // LANES, tokens, LANES), lambda j: (j, 0, 0, 0))),
            (w_qkv, pl.BlockSpec((width, width), lambda j: (0, j))),
            (x, whole),
            (gain[None], full(1, width)),
            (drb, full(*drb.shape)),
            (back, full(rows * WINDOW, width)),
        ],
        [((tokens, width), F32, whole)],
        [pltpu.VMEM((tokens, width), F32)],
        us=8,
        after=after,
    )[0]


def rim_grad_kernel(drim_ref, wk_ref, wv_ref, x_ref, gain_ref, out_ref):
    grad = dot(side_by_side(drim_ref.at[0]), wk_ref[...], 1, 1)
    grad += dot(side_by_side(drim_ref.at[1]), wv_ref[...], 1, 1)
    out_ref[...] = norm_back(grad, x_ref[...].astype(F32), gain_ref[...]).astype(BF16)


def rim_grad(drim, w_qkv, x, gain, after=()):
    rim, width = x.shape
    part = lambda k: pl.BlockSpec((width, width), lambda j: (0, k))
    return launch(
        rim_grad_kernel,
        "rim_grad",
        (1,),
        [],
        [
            (drim, full(*drim.shape)),
            (w_qkv, part(1)),
            (w_qkv, part(2)),
            (x, full(rim, width)),
            (gain[None], full(1, width)),
        ],
        [((rim, width), BF16, full(rim, width))],
        us=8,
        after=after,
    )[0]


def add_kernel(facts_ref, *refs, bits):
    count = len(bits)
    for k, bit in enumerate(bits):
        keep_ref, got_ref = refs[2 * k : 2 * k + 2]
        outs = refs[2 * count + 2 * k : 2 * count + 2 * k + 2]
        for out_ref, index in zip(outs, (1 - facts_ref[bit], facts_ref[bit])):
            out_ref[...] = (keep_ref[:, index].astype(F32) + got_ref[:, index].astype(F32)).astype(BF16)


def add_and_cut(facts, items, after=()):
    inputs, outputs = [], []
    for keep, got, _ in items:
        kinds, rows, columns = keep.shape
        cut = lambda value: value.reshape(kinds, 2, rows // 2, columns)
        spec = pl.BlockSpec((kinds, 2, rows // 2, columns // 2), lambda j, *_: (0, 0, 0, j))
        inputs += [(cut(keep), spec), (cut(got), spec)]
        part = pl.BlockSpec((kinds, rows // 2, columns // 2), lambda j, *_: (0, 0, j))
        outputs += [((kinds, rows // 2, columns), BF16, part)] * 2
    kernel = functools.partial(add_kernel, bits=[bit for _, _, bit in items])
    parts = launch(kernel, "add_and_cut", (2,), [facts], inputs, outputs, us=8, after=after)
    return [(parts[2 * k], parts[2 * k + 1]) for k in range(len(items))]


def log2(count):
    return count.bit_length() - 1


def stage_orders(n_dp, n_seq, flavour):
    dp = [("dp", bit) for bit in range(1, log2(n_dp))]
    if flavour:
        dp = dp[::-1]
    seq = [("seq", bit) for bit in range(log2(n_seq))]
    return dp + seq, seq[:1] + dp + seq[1:]


def row_bits(n_dp, n_seq):
    return [("seq", bit) for bit in reversed(range(log2(n_seq)))] + [
        ("dp", bit) for bit in reversed(range(log2(n_dp)))
    ]


def block_places(n_dp, n_seq, flavour):
    bits, orders = row_bits(n_dp, n_seq), stage_orders(n_dp, n_seq, flavour)
    count = n_dp * n_seq
    tables = []
    for core in range(2):
        table = []
        for block in range(count):
            value = {step: (block >> (len(bits) - 1 - k)) & 1 for k, step in enumerate(bits)}
            owner = value[("dp", 0)]
            place = 0
            for step in orders[owner]:
                place = place * 2 + value[step]
            table.append(place + (count // 2 if owner == core else 0))
        tables.append(np.array(table, np.int32))
    return tables


def swap_pairs(n_dp, n_seq, steps):
    pairs = []
    for d in range(n_dp):
        for s in range(n_seq):
            axis, bit = steps[d % 2]
            there = (d ^ (1 << bit), s) if axis == "dp" else (d, s ^ (1 << bit))
            pairs.append((d * n_seq + s, there[0] * n_seq + there[1]))
    return pairs


def swap(value, steps):
    n_dp, n_seq = lax.axis_size("dp"), lax.axis_size("seq")
    return lax.ppermute(value, ("dp", "seq"), swap_pairs(n_dp, n_seq, steps))


def gather_steps(n_dp):
    dims = [("dp", bit) for bit in range(1, log2(n_dp))]
    return list(zip(dims[::-1], dims))


def stage_fact(n_dp, n_seq, flavour, stage):
    return 3 + flavour * (log2(n_dp * n_seq) - 1) + stage


def gather_fact(n_dp, n_seq, step):
    return 3 + 2 * (log2(n_dp * n_seq) - 1) + step


def places_fact(n_dp, n_seq, flavour, count):
    return gather_fact(n_dp, n_seq, log2(n_dp)) + flavour * count


def facts_table(n_dp, n_seq, group, places):
    table = []
    for d in range(n_dp):
        for s in range(n_seq):
            core = d & 1
            bit = lambda steps: ((d if steps[core][0] == "dp" else s) >> steps[core][1]) & 1
            row = [core, s, s * group]
            for flavour in range(2):
                row += [bit(steps) for steps in zip(*stage_orders(n_dp, n_seq, flavour))]
            row += [bit(steps) for steps in gather_steps(n_dp)] + [0]
            assert len(row) == places_fact(n_dp, n_seq, 0, 0)
            for flavour in range(2):
                row += list(places[flavour][core])
            table.append(row)
    return np.array(table, np.int32)


CORE = (("dp", 0), ("dp", 0))


class Chunk:
    def __init__(self, flavour):
        self.sizes = lax.axis_size("dp"), lax.axis_size("seq")
        self.flavour = flavour
        self.stages = list(zip(*stage_orders(*self.sizes, flavour)))
        self.done = 0

    def bit(self):
        return stage_fact(*self.sizes, self.flavour, self.done)

    def between_cores(self, *parts):
        self.got = [swap(part, CORE) for part in parts]

    def go(self, send, keep):
        self.keep = keep
        self.got = swap(send, self.stages[self.done])
        self.done += 1

    @property
    def last(self):
        return self.done == len(self.stages)


def advance(facts, *chunks, after=()):
    parts = add_and_cut(facts, [(chunk.keep, chunk.got, chunk.bit()) for chunk in chunks], after=after)
    for chunk, (send, keep) in zip(chunks, parts):
        chunk.go(send, keep)
    return parts[0][0]


def finish_kernel(*refs):
    out_ref, first = refs[-1], 0
    for keep_ref, got_ref in zip(refs[:-1:2], refs[1:-1:2]):
        columns = keep_ref.shape[2]
        total = keep_ref[...].astype(F32) + got_ref[...].astype(F32)
        out_ref[:, :, first : first + columns] = total.astype(BF16)
        first += columns


def finish(*chunks, us=8, after=()):
    kinds, part, _ = chunks[0].keep.shape
    inputs = [(array, full(*array.shape)) for chunk in chunks for array in (chunk.keep, chunk.got)]
    shape = (kinds, part, sum(chunk.keep.shape[2] for chunk in chunks))
    return launch(finish_kernel, "finish", (1,), [], inputs, [(shape, BF16, full(*shape))], us=us, after=after)[0]


def join_kernel(facts_ref, value_ref, got_ref, out_ref, *, bit):
    count = value_ref.shape[1]
    first = facts_ref[bit] * count
    out_ref[:, pl.ds(first, count)] = value_ref[...]
    out_ref[:, pl.ds(count - first, count)] = got_ref[...]


class Gather:
    def __init__(self, facts, value):
        self.facts = facts
        n_dp = lax.axis_size("dp")
        self.dims = [("dp", bit) for bit in range(1, log2(n_dp))]
        self.steps = gather_steps(n_dp)
        self.kinds, self.part, self.columns = value.shape
        self.value = value[:, None]
        self.done = 0
        self.send()

    @property
    def last(self):
        return self.done == len(self.steps)

    def send(self):
        self.got = swap(self.value, CORE if self.last else self.steps[self.done])

    def step(self, us=8, after=()):
        bit = gather_fact(lax.axis_size("dp"), lax.axis_size("seq"), self.done)
        kinds, count, part, columns = self.value.shape
        tile = columns // 2
        spec = lambda count: pl.BlockSpec((kinds, count, part, tile), lambda j, *_: (0, 0, 0, j))
        (self.value,) = launch(
            functools.partial(join_kernel, bit=bit),
            "join",
            (2,),
            [self.facts],
            [(self.value, spec(count)), (self.got, spec(count))],
            [((kinds, 2 * count, part, columns), BF16, spec(2 * count))],
            us=us,
            after=after,
        )
        self.done += 1
        self.send()
        return self.value

    def whole(self):
        dims = self.dims
        core = lax.axis_index("dp") & 1
        halves = []
        for which, order in enumerate((dims[::-1], dims)):
            half = jnp.where(core == which, self.value, self.got)
            half = half.reshape((self.kinds,) + (2,) * len(dims) + (self.part, self.columns))
            wanted = [1 + order[::-1].index(step) for step in dims[::-1]]
            halves.append(half.transpose([0] + wanted + [len(dims) + 1, len(dims) + 2]))
        whole = jnp.stack(halves, axis=len(dims) + 1)
        return whole.reshape(self.kinds, lax.axis_size("dp") * self.part, self.columns)


def natural_rows(facts_ref, own_ref, got_ref, kind, step, columns):
    pieces = []
    for x in range(2):
        for which in range(2):
            index = x * 2 + step if which == 0 else step * 2 + x
            own, got = own_ref[kind, index, :, columns], got_ref[kind, index, :, columns]
            pieces.append(jnp.where(facts_ref[CORE_INDEX] == which, own, got))
    return jnp.concatenate(pieces, axis=0).astype(F32)


def row_sums(value):
    total = jnp.sum(value, axis=1, keepdims=True)
    return jnp.broadcast_to(total, (total.shape[0], LANES)).T[:1, :]


def put_ff_kernel(facts_ref, own_ref, got_ref, w_ref, gain_ref, gate_up_ref, down_ref, dgain_ref):
    step = pl.program_id(0)
    rows = lambda kind: natural_rows(facts_ref, own_ref, got_ref, kind, step, slice(0, FF))
    down_ref[...] = rows(0).T
    gate, up = rows(1), rows(2)
    gate_up_ref[:, :FF] = gate
    gate_up_ref[:, FF:] = up
    weight = w_ref[...].astype(F32)
    total = row_sums(gate * weight[:, :FF]) + row_sums(up * weight[:, FF:])
    dgain_ref[...] = total / gain_ref[...]


def put_ff(gather, w_gate_up, gain, after=()):
    kept = 8 * gather.part
    half = kept // 2
    whole = full(*gather.value.shape)
    return launch(
        put_ff_kernel,
        "put_ff",
        (2,),
        [gather.facts],
        [
            (gather.value, whole),
            (gather.got, whole),
            (w_gate_up, pl.BlockSpec((half, 2 * FF), lambda j, facts: (2 * facts[SEQ_INDEX] + j, 0))),
            (gain[None], pl.BlockSpec((1, half), lambda j, facts: (0, 2 * facts[SEQ_INDEX] + j))),
        ],
        [
            ((kept, 2 * FF), F32, pl.BlockSpec((half, 2 * FF), lambda j, *_: (j, 0))),
            ((FF, kept), F32, pl.BlockSpec((FF, half), lambda j, *_: (0, j))),
            ((1, kept), F32, pl.BlockSpec((1, half), lambda j, *_: (0, j))),
        ],
        us=8,
        after=after,
    )


def put_att_kernel(facts_ref, own_ref, got_ref, w_ref, gain_ref, qkv_ref, out_ref, dgain_ref):
    step = pl.program_id(0)
    width = out_ref.shape[1]
    out_ref[...] = natural_rows(facts_ref, own_ref, got_ref, 0, step, slice(0, width))
    qkv = natural_rows(facts_ref, own_ref, got_ref, 0, step, slice(width, 4 * width))
    qkv_ref[...] = qkv
    dgain_ref[...] = row_sums(qkv * w_ref[...].astype(F32)) / gain_ref[...]


def put_att(gather, w_qkv, gain, after=()):
    kept = 8 * gather.part
    half, width = kept // 2, gather.columns // 4
    whole = full(*gather.value.shape)
    return launch(
        put_att_kernel,
        "put_att",
        (2,),
        [gather.facts],
        [
            (gather.value, whole),
            (gather.got, whole),
            (w_qkv, pl.BlockSpec((half, 3 * width), lambda j, facts: (2 * facts[SEQ_INDEX] + j, 0))),
            (gain[None], pl.BlockSpec((1, half), lambda j, facts: (0, 2 * facts[SEQ_INDEX] + j))),
        ],
        [
            ((kept, 3 * width), F32, pl.BlockSpec((half, 3 * width), lambda j, *_: (j, 0))),
            ((kept, width), F32, pl.BlockSpec((half, width), lambda j, *_: (j, 0))),
            ((1, kept), F32, pl.BlockSpec((1, half), lambda j, *_: (0, j))),
        ],
        us=8,
        after=after,
    )


def place_rows(turned, places):
    count = places.shape[0]
    blocks = turned.reshape((count, turned.shape[0] // count) + turned.shape[1:])
    return jnp.zeros_like(blocks).at[places].set(blocks).reshape(turned.shape)


def shifted(value, axis, steps):
    count = lax.axis_size(axis)
    leading, last = (max(0, -steps), min(count, count - steps))
    return lax.ppermute(value, axis, [(source, source + steps) for source in range(leading, last)])


def per_device(inputs, w_qkv, w_out, w_gate_up, w_down, gain_attn, gain_mlp, doc_start, cotangent):
    n_dp, n_seq = lax.axis_size("dp"), lax.axis_size("seq")
    rows, group, width = inputs.shape
    tokens = rows * group
    slab = width // (n_dp * n_seq)
    places = [block_places(n_dp, n_seq, flavour) for flavour in range(2)]
    ordered = slab % 16 == 0
    if not ordered:
        slab = 32
    blocks = width // slab
    listed = places if ordered else [[np.arange(blocks)] * 2] * 2
    table = facts_table(n_dp, n_seq, group, listed)
    device = lax.axis_index("dp") * n_seq + lax.axis_index("seq")
    facts = lax.dynamic_index_in_dim(jnp.asarray(table), device, axis=0, keepdims=False)
    put = [places_fact(n_dp, n_seq, flavour, blocks) for flavour in range(2)]
    core = lax.axis_index("dp") & 1

    def in_order(turned, flavour):
        if ordered:
            return turned
        return place_rows(turned, jnp.where(core == 0, *places[flavour]))

    x = inputs.reshape(tokens, width)
    dy = cotangent.reshape(tokens, width)

    tails = [(row + 1) * group for row in range(rows)]
    qkv, one_turned, x_tail = norm_matmul(x, gain_attn, w_qkv, 0, facts, put[0], slab, tails)
    x_rim = shifted(x_tail, "seq", 1)
    dy_turned = turn(dy, facts, put[1], slab, after=[qkv])
    kv_rim, rim_turned, _ = norm_matmul(
        x_rim, gain_attn, w_qkv, width, facts, put[0], slab, [WINDOW], after=[dy_turned]
    )
    att, att_turned = attend(qkv, kv_rim, doc_start, facts, put[0], slab)
    resid, normed_two, two_turned = out_proj(att, w_out, x, gain_mlp, facts, put[1], slab)
    one_turned, rim_turned, att_turned = [in_order(turned, 0) for turned in (one_turned, rim_turned, att_turned)]
    two_turned, dy_turned = [in_order(turned, 1) for turned in (two_turned, dy_turned)]

    def feed(first, count, total=None, end=None, after=()):
        hidden, dgu, *rest = feed_forward(
            normed_two, dy, dy_turned, two_turned, w_gate_up, w_down, first, count, total, end, after
        )
        chunk = Chunk(1)
        chunk.between_cores(*rest[:3])
        return hidden, dgu, chunk, rest[3:]

    def keep_ff(chunk, hidden, dgu, after=()):
        send, keep = ff_grad(facts, chunk.bit(), dy_turned, two_turned, hidden, dgu, chunk.got, after=after)
        chunk.go(send, keep)
        return send

    count = FF_CHUNKS[0]
    hidden_one, dgu_one, one, (total,) = feed(0, count)
    token = keep_ff(one, hidden_one, dgu_one)
    hidden_two, dgu_two, two, (drb, da) = feed(count, FF_CHUNKS[1], total, (resid, gain_mlp, w_out), after=[token])
    token = advance(facts, one, after=[da])
    token = keep_ff(two, hidden_two, dgu_two, after=[token])
    dqkv, drim = attend_back(qkv, kv_rim, doc_start, facts, da, after=[token])
    att = Chunk(0)
    grads = (facts, att_turned, one_turned, rim_turned, drb, dqkv, drim)
    sends = att_grad(*grads, after=[one.got])
    att.between_cores(*sends)
    token = advance(facts, one, two, after=sends)
    send, keep = att_grad(*grads, att.bit(), att.got, after=[token])
    att.go(send[None], keep[None])
    token = advance(facts, one, two, after=[send])
    back = rim_grad(drim, w_qkv, x_rim, gain_attn, after=[token])
    back_got = shifted(back, "seq", -1)
    outputs = ff_out([hidden_one, hidden_two], w_down, resid, after=[back])
    token = advance(facts, att, two, after=[outputs, one.got])
    while not (one.last and two.last):
        token = advance(facts, *(chunk for chunk in (one, two) if not chunk.last), after=[token])
    grad_inputs = input_grad(dqkv, w_qkv, x, gain_attn, drb, back_got, rows, group, after=[token])
    token = advance(facts, att, after=[grad_inputs])
    gather_ff = Gather(facts, finish(one, two, after=[token]))
    token = gather_ff.value
    while not att.last:
        token = advance(facts, att, after=[token])
    token = gather_ff.step(after=[token])
    gather = Gather(facts, finish(att, after=[token]))
    if ordered and n_dp == 8:
        token = gather_ff.step(after=[gather.value])
        token = gather.step(us=24, after=[token])
        total_gate_up, turned_down, gain_two = put_ff(gather_ff, w_gate_up, gain_mlp, after=[token])
        total_down = turned_down.T
        gather.step(after=[total_gate_up])
        total_qkv, total_out, gain_one = put_att(gather, w_qkv, gain_attn)
        gain_one, gain_two = gain_one[0], gain_two[0]
    else:
        for both in (gather_ff, gather):
            while not both.last:
                both.step()
        total_ff = gather_ff.whole()
        rest = gather.whole()[0]
        total_down, total_gate, total_up = [total_ff[kind, :, :FF] for kind in range(3)]
        total_down = total_down.astype(F32)
        total_gate_up = jnp.concatenate([total_gate, total_up], axis=1).astype(F32)
        total_out = rest[:, :width].astype(F32)
        total_qkv = rest[:, width:].astype(F32)
        kept = total_qkv.shape[0]
        first_row = lax.axis_index("seq") * kept

        def gain_total(total, weight, gain):
            mine = lax.dynamic_slice_in_dim(weight, first_row, kept, axis=0).astype(F32)
            return jnp.sum(total * mine, axis=1) / lax.dynamic_slice_in_dim(gain, first_row, kept)

        gain_one = gain_total(total_qkv, w_qkv, gain_attn)
        gain_two = gain_total(total_gate_up, w_gate_up, gain_mlp)

    return (
        outputs.reshape(rows, group, width),
        grad_inputs.reshape(rows, group, width),
        total_qkv,
        total_out,
        total_gate_up,
        total_down,
        gain_one,
        gain_two,
    )


def solution(mesh):
    in_specs = (
        P("dp", "seq", None),
        P(),
        P(),
        P(),
        P(),
        P(),
        P(),
        P("dp", "seq"),
        P("dp", "seq", None),
    )
    out_specs = (
        P("dp", "seq", None),
        P("dp", "seq", None),
        P("seq", None),
        P("seq", None),
        P("seq", None),
        P("seq", None),
        P("seq"),
        P("seq"),
    )
    return jax.shard_map(
        per_device, mesh=mesh, in_specs=in_specs, out_specs=out_specs, check_vma=False
    )
```

profile of v0, /device:TPU:0, one launch (start us, length us, event | category | flops | bytes accessed | tf_op | source)
XLA Modules:
  0.0 329.2 jit_solution(1533450096765000388)
XLA Ops:
  0.6 1.2 dynamic-slice_bitcast_fusion.refs_0_
  1.8 12.7 %norm_matmul.2 = (bf16[24,1024,128]{2,1,0:T(8,128)(2,1)}, bf16[1024,1024]{1,0:T(8,128)(2,1)}, bf16[128,1024]{1,0:T(8,128)(2,1)}) custom-call(s32[78]{0:T(128)} %dynamic-slice_bitcast_fusion.refs_0_, bf16[1024,1024]{1,0:T(8,128)(2,1)} %bitcast.43, f32[1,1024]{1,0:T(1,128)} %bitcast.53, bf16[1024,3072]{1,0:T(8,128)(2,1)} %refs_3_.7), custom_call_target="tpu_custom_call" | custom-call | flops 8800000000 | bytes 170434 | tf_op jit(solution)/shard_map/norm_matmul/pallas_call | solution.py:46
  14.5 6.1 %collective-permute-start = (bf16[128,1024]{1,0:T(8,128)(2,1)}, bf16[128,1024]{1,0:T(8,128)(2,1)}, u32[]{:S(2)}, u32[]{:S(2)}) collective-permute-start(bf16[128,1024]{1,0:T(8,128)(2,1)} %get-tuple-element.68), channel_id=1, source_target_pairs={{0,1},{1,2},{2,3},{4,5},{5,6},{6,7},{8,9},{9,10},{10,11},{12,13},{... | collective-permute-start | bytes 786440 | tf_op jit(solution)/shard_map/ppermute | solution.py:999
  20.7 3.6 %turn.1.refs_4_.refs_2_.refs_1_ = bf16[1024,1024]{1,0:T(8,128)(2,1)} custom-call(s32[78]{0:T(128)} %dynamic-slice_bitcast_fusion.refs_0_, bf16[1024,1024]{1,0:T(8,128)(2,1)} %bitcast.36, bf16[24,1024,128]{2,1,0:T(8,128)(2,1)} %get-tuple-element.67.refs_2_.refs_3_.refs_4_), custom_call_target="tpu_custom_call" | custom-call | flops 8800000000 | bytes 41943 | tf_op jit(solution)/shard_map/turn/pallas_call | solution.py:46
  24.3 1.0 collective-permute-done.refs_1_.refs_3_
  25.3 4.2 %norm_matmul.3 = (bf16[16,128,128]{2,1,0:T(8,128)(2,1)}, bf16[1024,128]{1,0:T(8,128)(2,1)}, bf16[64,1024]{1,0:T(8,128)(2,1)}) custom-call(s32[78]{0:T(128)} %dynamic-slice_bitcast_fusion.refs_0_, bf16[128,1024]{1,0:T(8,128)(2,1)} %collective-permute-done.refs_1_.refs_3_, f32[1,1024]{1,0:T(1,128)} %bitcast.54, bf16[1024,3072]{1,0:T(8,128)(2,1)} %refs_3_.7, ...), custom_call_target="tpu_custom_call" | custom-call | flops 8800000000 | bytes 74752 | tf_op jit(solution)/shard_map/norm_matmul/pallas_call | solution.py:46
  29.5 10.6 %attend.1 = (bf16[8,1024,128]{2,1,0:T(8,128)(2,1)}, bf16[1024,1024]{1,0:T(8,128)(2,1)}) custom-call(s32[78]{0:T(128)} %dynamic-slice_bitcast_fusion.refs_0_, s32[2,512]{1,0:T(2,128)} %refs_1_.5, bf16[24,1024,128]{2,1,0:T(8,128)(2,1)} %get-tuple-element.67.refs_2_.refs_3_.refs_4_, bf16[24,1024,128]{2,1,0:T(8,128)(2,1)} %get-tuple-element.67.refs_2_.refs_3_.refs_4_, ...), custom_call_target="tpu_custom_call" | custom-call | flops 8800000000 | bytes 241213 | tf_op jit(solution)/shard_map/attend/pallas_call | solution.py:46
  40.1 8.0 %out_proj.1 = (bf16[1024,1024]{1,0:T(8,128)(2,1)}, bf16[1024,1024]{1,0:T(8,128)(2,1)}, bf16[1024,1024]{1,0:T(8,128)(2,1)}) custom-call(s32[78]{0:T(128)} %dynamic-slice_bitcast_fusion.refs_0_, bf16[8,1024,128]{2,1,0:T(8,128)(2,1)} %get-tuple-element.70.refs_1_, bf16[1024,1024]{1,0:T(8,128)(2,1)} %refs_12_.1, bf16[1024,1024]{1,0:T(8,128)(2,1)} %bitcast.44, ...), custom_call_target="tpu_custom_call" | custom-call | flops 8800000000 | bytes 125870 | tf_op jit(solution)/shard_map/out_proj/pallas_call | solution.py:46
  48.1 30.2 %feed_forward.2 = (bf16[1024,1536]{1,0:T(8,128)(2,1)}, bf16[2,1024,1536]{2,1,0:T(8,128)(2,1)}, bf16[512,1536]{1,0:T(8,128)(2,1)}, bf16[512,1536]{1,0:T(8,128)(2,...) custom-call(bf16[1024,1024]{1,0:T(8,128)(2,1)} %get-tuple-element.71.refs_0_, bf16[1024,1024]{1,0:T(8,128)(2,1)} %bitcast.37, ...), custom_call_target="tpu_custom_call" | custom-call | flops 8800000000 | bytes 774635 | tf_op jit(solution)/shard_map/feed_forward/pallas_call | solution.py:46
  78.4 0.5 collective-permute-start.2
  79.0 3.2 collective-permute-done.1.refs_5_
  82.2 2.2 collective-permute-done.2.refs_6_
  84.4 2.2 collective-permute-done.3.refs_7_
  86.7 12.1 %ff_grad.2 = (bf16[3,256,1536]{2,1,0:T(8,128)(2,1)}, bf16[3,256,1536]{2,1,0:T(8,128)(2,1)}) custom-call(s32[78]{0:T(128)} %dynamic-slice_bitcast_fusion.refs_0_, bf16[1024,1024]{1,0:T(8,128)(2,1)} %turn.1.refs_4_.refs_2_.refs_1_, bf16[1024,1024]{1,0:T(8,128)(2,1)} %get-tuple-element.72.refs_3_.refs_2_, bf16[1024,1536]{1,0:T(8,128)(2,1)} %get-tuple-element.73.refs_3_.refs_0_, ...), custom_call_target="tpu_custom_call" | custom-call | flops 8800000000 | bytes 230686 | tf_op jit(solution)/shard_map/ff_grad/pallas_call | solution.py:46
  98.7 1.5 collective-permute-start.7
  100.2 32.1 %feed_forward.3 = (bf16[1024,1280]{1,0:T(8,128)(2,1)}, bf16[2,1024,1280]{2,1,0:T(8,128)(2,1)}, bf16[512,1280]{1,0:T(8,128)(2,1)}, bf16[512,1280]{1,0:T(8,128)(2,...) custom-call(bf16[1024,1024]{1,0:T(8,128)(2,1)} %get-tuple-element.71.refs_0_, ...), custom_call_target="tpu_custom_call" | custom-call | flops 8800000000 | bytes 834969 | tf_op jit(solution)/shard_map/feed_forward/pallas_call | solution.py:46
  132.4 0.9 collective-permute-start.4
  133.3 0.4 collective-permute-start.6
  133.8 4.3 %add_and_cut.6 = (bf16[3,128,1536]{2,1,0:T(8,128)(2,1)}, bf16[3,128,1536]{2,1,0:T(8,128)(2,1)}) custom-call(s32[78]{0:T(128)} %dynamic-slice_bitcast_fusion.refs_0_, bf16[3,2,128,1536]{3,2,1,0:T(8,128)(2,1)} %bitcast.60, bf16[3,2,128,1536]{3,2,1,0:T(8,128)(2,1)} %bitcast.7.refs_2_, bf16[8,1024,128]{2,1,0:T(8,128)(2,1)} %get-tuple-element.82.refs_3_.refs_7_), custom_call_target="tpu_custom_call" | custom-call | flops 8800000000 | bytes 70778 | tf_op jit(solution)/shard_map/add_and_cut/pallas_call | solution.py:46
  138.1 1.5 collective-permute-start.8
  139.6 0.4 collective-permute-done.6.refs_7_
  140.0 11.1 %ff_grad.3 = (bf16[3,256,1280]{2,1,0:T(8,128)(2,1)}, bf16[3,256,1280]{2,1,0:T(8,128)(2,1)}) custom-call(s32[78]{0:T(128)} %dynamic-slice_bitcast_fusion.refs_0_, bf16[1024,1024]{1,0:T(8,128)(2,1)} %turn.1.refs_4_.refs_2_.refs_1_, bf16[1024,1024]{1,0:T(8,128)(2,1)} %get-tuple-element.72.refs_3_.refs_2_, bf16[1024,1280]{1,0:T(8,128)(2,1)} %get-tuple-element.81.refs_3_.refs_1_, ...), custom_call_target="tpu_custom_call" | custom-call | flops 8800000000 | bytes 199229 | tf_op jit(solution)/shard_map/ff_grad/pallas_call | solution.py:46
  151.2 1.5 collective-permute-start.9
  152.7 16.4 %attend_back.1 = (bf16[3,8,1024,128]{3,2,1,0:T(8,128)(2,1)}, bf16[2,8,128,128]{3,2,1,0:T(8,128)(2,1)}) custom-call(s32[78]{0:T(128)} %dynamic-slice_bitcast_fusion.refs_0_, s32[2,512]{1,0:T(2,128)} %refs_1_.5, bf16[24,1024,128]{2,1,0:T(8,128)(2,1)} %get-tuple-element.67.refs_2_.refs_3_.refs_4_, ...), custom_call_target="tpu_custom_call" | custom-call | flops 8800000000 | bytes 288399 | tf_op jit(solution)/shard_map/attend_back/pallas_call | solution.py:46
  169.1 11.9 %att_grad.2 = (bf16[512,1024]{1,0:T(8,128)(2,1)}, bf16[512,1024]{1,0:T(8,128)(2,1)}, bf16[512,1024]{1,0:T(8,128)(2,1)}, bf16[512,1024]{1,0:T(8,128)(2,1)}) custom-call(s32[78]{0:T(128)} %dynamic-slice_bitcast_fusion.refs_0_, bf16[1024,1024]{1,0:T(8,128)(2,1)} %get-tuple-element.93.refs_1_, bf16[1024,1024]{1,0:T(8,128)(2,1)} %get-tuple-element.94.refs_2_, ...), custom_call_target="tpu_custom_call" | custom-call | flops 8800000000 | bytes 175636 | tf_op jit(solution)/shard_map/att_grad/pallas_call | solution.py:46
  181.0 0.4 collective-permute-start.12
  182.0 4.9 %add_and_cut.7 = (bf16[3,64,1536]{2,1,0:T(8,128)(2,1)}, bf16[3,64,1536]{2,1,0:T(8,128)(2,1)}, bf16[3,128,1280]{2,1,0:T(8,128)(2,1)}, bf16[3,128,1280]{2,1,0:T(8,128)(2,1)}) custom-call(s32[78]{0:T(128)} %dynamic-slice_bitcast_fusion.refs_0_, bf16[3,2,64,1536]{3,2,1,0:T(8,128)(2,1)} %bitcast.63, bf16[3,2,64,1536]{3,2,1,0:T(8,128)(2,1)} %bitcast.9.refs_2_, ...), custom_call_target="tpu_custom_call" | custom-call | flops 8800000000 | bytes 94371 | tf_op jit(solution)/shard_map/add_and_cut/pallas_call | solution.py:46
  186.9 1.5 collective-permute-start.11
  188.4 1.0 collective-permute-start.10
  189.4 12.1 %att_grad.3 = (bf16[256,4096]{1,0:T(8,128)(2,1)}, bf16[256,4096]{1,0:T(8,128)(2,1)}) custom-call(s32[78]{0:T(128)} %dynamic-slice_bitcast_fusion.refs_0_, bf16[1024,1024]{1,0:T(8,128)(2,1)} %get-tuple-element.93.refs_1_, bf16[1024,1024]{1,0:T(8,128)(2,1)} %get-tuple-element.94.refs_2_, bf16[1024,128]{1,0:T(8,128)(2,1)} %get-tuple-element.95.refs_3_, ...), custom_call_target="tpu_custom_call" | custom-call | flops 8800000000 | bytes 217579 | tf_op jit(solution)/shard_map/att_grad/pallas_call | solution.py:46
  201.5 0.6 collective-permute-start.17
  202.1 5.2 %collective-permute-done.11 = bf16[3,128,1280]{2,1,0:T(8,128)(2,1)} collective-permute-done((bf16[3,128,1280]{2,1,0:T(8,128)(2,1)}, bf16[3,128,1280]{2,1,0:T(8,128)(2,1)}, u32[]{:S(2)}, u32[]{:S(2)}) %collective-permute-start.11) | collective-permute-done | bytes 983072 | tf_op jit(solution)/shard_map/ppermute | solution.py:761
  207.3 3.5 %add_and_cut.8 = (bf16[3,32,1536]{2,1,0:T(8,128)(2,1)}, bf16[3,32,1536]{2,1,0:T(8,128)(2,1)}, bf16[3,64,1280]{2,1,0:T(8,128)(2,1)}, bf16[3,64,1280]{2,1,0:T(8,128)(2,1)}) custom-call(s32[78]{0:T(128)} %dynamic-slice_bitcast_fusion.refs_0_, bf16[3,2,32,1536]{3,2,1,0:T(8,128)(2,1)} %bitcast.66, bf16[3,2,32,1536]{3,2,1,0:T(8,128)(2,1)} %bitcast.13.refs_2_, ...), custom_call_target="tpu_custom_call" | custom-call | flops 8800000000 | bytes 47185 | tf_op jit(solution)/shard_map/add_and_cut/pallas_call | solution.py:46
  210.7 1.4 collective-permute-start.18
  212.1 2.6 collective-permute-start.19
  214.7 4.8 %rim_grad.1.refs_4_ = bf16[128,1024]{1,0:T(8,128)(2,1)} custom-call(bf16[2,8,128,128]{3,2,1,0:T(8,128)(2,1)} %get-tuple-element.90.refs_6_.refs_0_, bf16[1024,3072]{1,0:T(8,128)(2,1)} %refs_3_.7, bf16[1024,3072]{1,0:T(8,128)(2,1)} %refs_3_.7, bf16[128,1024]{1,0:T(8,128)(2,1)} %collective-permute-done.refs_1_.refs_3_, f32[1,1024]{1,0:T(1,128)} %bitcast.55, ...), custom_call_target="tpu_custom_call" | custom-call | flops 8800000000 | bytes 136355 | tf_op jit(solution)/shard_map/rim_grad/pallas_call | solution.py:46
  219.5 1.3 collective-permute-start.16
  220.8 11.2 %ff_out.1.refs_5_ = bf16[1024,1024]{1,0:T(8,128)(2,1)} custom-call(bf16[1024,1536]{1,0:T(8,128)(2,1)} %get-tuple-element.73.refs_3_.refs_0_, bf16[1024,1280]{1,0:T(8,128)(2,1)} %get-tuple-element.81.refs_3_.refs_1_, bf16[2752,1024]{1,0:T(8,128)(2,1)} %bitcast.35, bf16[1024,1024]{1,0:T(8,128)(2,1)} %get-tuple-element.75.refs_10_.refs_3_, ...), custom_call_target="tpu_custom_call" | custom-call | flops 1100000000 | bytes 155975 | tf_op jit(solution)/shard_map/ff_out/pallas_call | solution.py:46
  232.0 3.0 collective-permute-done.17
  235.0 4.4 %add_and_cut.9 = (bf16[1,128,4096]{2,1,0:T(8,128)(2,1)}, bf16[1,128,4096]{2,1,0:T(8,128)(2,1)}, bf16[3,32,1280]{2,1,0:T(8,128)(2,1)}, bf16[3,32,1280]{2,1,0:T(8,128)(2,1)}) custom-call(s32[78]{0:T(128)} %dynamic-slice_bitcast_fusion.refs_0_, bf16[1,2,128,4096]{3,2,1,0:T(8,128)(2,1)} %bitcast.61, bf16[1,2,128,4096]{3,2,1,0:T(8,128)(2,1)} %bitcast.19.refs_2_, ...), custom_call_target="tpu_custom_call" | custom-call | flops 8800000000 | bytes 77660 | tf_op jit(solution)/shard_map/add_and_cut/pallas_call | solution.py:46
  239.4 0.9 collective-permute-start.20
  240.2 3.0 collective-permute-start.22
  243.3 15.4 %input_grad.1.refs_3_ = f32[1024,1024]{1,0:T(8,128)} custom-call(bf16[3,8,1024,128]{3,2,1,0:T(8,128)(2,1)} %get-tuple-element.97.refs_5_.refs_0_, bf16[1024,3072]{1,0:T(8,128)(2,1)} %refs_3_.7, bf16[1024,1024]{1,0:T(8,128)(2,1)} %bitcast.45, f32[1,1024]{1,0:T(1,128)} %bitcast.56, bf16[8,1024,128]{2,1,0:T(8,128)(2,1)} %get-tuple-element.96.refs_4_, ...), custom_call_target="tpu_custom_call" | custom-call | flops 8800000000 | bytes 212377 | tf_op jit(solution)/shard_map/input_grad/pallas_call | solution.py:46
  258.7 3.0 add_and_cut.10
  261.8 0.9 collective-permute-start.21
  262.7 2.1 finish.2
  264.8 1.2 collective-permute-start.24
  266.0 5.3 %collective-permute-done.21 = bf16[1,64,4096]{2,1,0:T(8,128)(2,1)} collective-permute-done((bf16[1,64,4096]{2,1,0:T(8,128)(2,1)}, bf16[1,64,4096]{2,1,0:T(8,128)(2,1)}, u32[]{:S(2)}, u32[]{:S(2)}) %collective-permute-start.21) | collective-permute-done | bytes 524320 | tf_op jit(solution)/shard_map/ppermute | solution.py:761
  271.3 2.6 add_and_cut.11
  273.9 5.1 %collective-permute-done.24.refs_2_ = bf16[3,1,32,2816]{3,2,1,0:T(8,128)(2,1)} collective-permute-done((bf16[3,1,32,2816]{3,2,1,0:T(8,128)(2,1)}, bf16[3,1,32,2816]{3,2,1,0:T(8,128)(2,1)}, u32[]{:S(2)}, u32[]{:S(2)}) %collective-permute-start.24) | collective-permute-done | bytes 540704 | tf_op jit(solution)/shard_map/ppermute | solution.py:761
  279.0 2.7 join.4.refs_2_.refs_1_
  281.7 0.5 collective-permute-start.26
  282.3 2.0 collective-permute-done.23.refs_1_
  284.3 1.8 finish.3
  286.1 0.8 collective-permute-start.25
  286.9 13.1 %collective-permute-done.26.refs_2_ = bf16[3,2,32,2816]{3,2,1,0:T(8,128)(2,1)} collective-permute-done((bf16[3,2,32,2816]{3,2,1,0:T(8,128)(2,1)}, bf16[3,2,32,2816]{3,2,1,0:T(8,128)(2,1)}, u32[]{:S(2)}, u32[]{:S(2)}) %collective-permute-start.26) | collective-permute-done | bytes 1081376 | tf_op jit(solution)/shard_map/ppermute | solution.py:761
  300.0 3.3 %join.5.refs_3_.refs_1_ = bf16[3,4,32,2816]{3,2,1,0:T(8,128)(2,1)} custom-call(s32[78]{0:T(128)} %dynamic-slice_bitcast_fusion.refs_0_, bf16[3,2,32,2816]{3,2,1,0:T(8,128)(2,1)} %join.4.refs_2_.refs_1_, bf16[3,2,32,2816]{3,2,1,0:T(8,128)(2,1)} %collective-permute-done.26.refs_2_, bf16[1,1,32,4096]{3,2,1,0:T(8,128)(2,1)} %bitcast.51), custom_call_target="tpu_custom_call" | custom-call | flops 8800000000 | bytes 43253 | tf_op jit(solution)/shard_map/join/pallas_call | solution.py:46
  303.3 2.7 collective-permute-start.28
  306.0 2.5 join.6.refs_5_.refs_1_
  308.5 1.5 collective-permute-start.27
  310.3 8.0 %put_ff.1 = (f32[256,5504]{1,0:T(8,128)}, f32[2752,256]{1,0:T(8,128)}, f32[1,256]{1,0:T(1,128)}) custom-call(s32[78]{0:T(128)} %dynamic-slice_bitcast_fusion.refs_0_, bf16[3,4,32,2816]{3,2,1,0:T(8,128)(2,1)} %join.5.refs_3_.refs_1_, bf16[3,4,32,2816]{3,2,1,0:T(8,128)(2,1)} %collective-permute-done.28.refs_2_, bf16[1024,5504]{1,0:T(8,128)(2,1)} %refs_3_.6, ...), custom_call_target="tpu_custom_call" | custom-call | flops 8800000000 | bytes 240568 | tf_op jit(solution)/shard_map/put_ff/pallas_call | solution.py:46
  318.2 2.7 join.7.refs_1_
  321.3 2.6 collective-permute-done.29.refs_2_
  324.0 4.9 %put_att.1 = (f32[256,3072]{1,0:T(8,128)}, f32[256,1024]{1,0:T(8,128)}, f32[1,256]{1,0:T(1,128)}) custom-call(s32[78]{0:T(128)} %dynamic-slice_bitcast_fusion.refs_0_, bf16[1,4,32,4096]{3,2,1,0:T(8,128)(2,1)} %join.7.refs_1_, bf16[1,4,32,4096]{3,2,1,0:T(8,128)(2,1)} %collective-permute-done.29.refs_2_, bf16[1024,3072]{1,0:T(8,128)(2,1)} %refs_3_.7, ...), custom_call_target="tpu_custom_call" | custom-call | flops 8800000000 | bytes 125880 | tf_op jit(solution)/shard_map/put_att/pallas_call | solution.py:46
  (26 shorter events, 1.5 us)
Async XLA Ops:
  14.5 10.8 %collective-permute-start = (bf16[128,1024]{1,0:T(8,128)(2,1)}, bf16[128,1024]{1,0:T(8,128)(2,1)}, u32[]{:S(2)}, u32[]{:S(2)}) collective-permute-start(bf16[128,1024]{1,0:T(8,128)(2,1)} %get-tuple-element.68), channel_id=1, source_target_pairs={{0,1},{1,2},{2,3},{4,5},{5,6},{6,7},{8,9},{9,10},{10,11},{12,13},{... | collective-permute-start | bytes 786440 | tf_op jit(solution)/shard_map/ppermute | solution.py:999
  78.3 3.8 %collective-permute-start.1 = (bf16[512,1536]{1,0:T(8,128)(2,1)}, bf16[512,1536]{1,0:T(8,128)(2,1)}, u32[]{:S(2)}, u32[]{:S(2)}) collective-permute-start(bf16[512,1536]{1,0:T(8,128)(2,1)} %get-tuple-element.77), channel_id=1, source_target_pairs={{0,4},{1,5},{2,6},{3,7},{4,0},{5,1},{6,2},{7,3},{8,12},{9,13},{10,... | collective-permute-start | bytes 4718600 | tf_op jit(solution)/shard_map/ppermute | solution.py:761
  78.4 6.0 %collective-permute-start.2 = (bf16[512,1536]{1,0:T(8,128)(2,1)}, bf16[512,1536]{1,0:T(8,128)(2,1)}, u32[]{:S(2)}, u32[]{:S(2)}) collective-permute-start(bf16[512,1536]{1,0:T(8,128)(2,1)} %get-tuple-element.78), channel_id=1, source_target_pairs={{0,4},{1,5},{2,6},{3,7},{4,0},{5,1},{6,2},{7,3},{8,12},{9,13},{10,... | collective-permute-start | bytes 4718600 | tf_op jit(solution)/shard_map/ppermute | solution.py:761
  78.9 7.7 %collective-permute-start.3 = (bf16[512,1536]{1,0:T(8,128)(2,1)}, bf16[512,1536]{1,0:T(8,128)(2,1)}, u32[]{:S(2)}, u32[]{:S(2)}) collective-permute-start(bf16[512,1536]{1,0:T(8,128)(2,1)} %get-tuple-element.79), channel_id=1, source_target_pairs={{0,4},{1,5},{2,6},{3,7},{4,0},{5,1},{6,2},{7,3},{8,12},{9,13},{10,... | collective-permute-start | bytes 4718600 | tf_op jit(solution)/shard_map/ppermute | solution.py:761
  98.7 35.0 %collective-permute-start.7 = (bf16[3,256,1536]{2,1,0:T(8,128)(2,1)}, bf16[3,256,1536]{2,1,0:T(8,128)(2,1)}, u32[]{:S(2)}, u32[]{:S(2)}) collective-permute-start(bf16[3,256,1536]{2,1,0:T(8,128)(2,1)} %get-tuple-element.80.refs_13_), channel_id=1, source_target_pairs={{0,16},{1,17},{2,18},{3,19},{4,5},{5,4},{6,7},{7,6},{8,24},{9,25},... | collective-permute-start | bytes 7077896 | tf_op jit(solution)/shard_map/ppermute | solution.py:761
  132.4 7.2 %collective-permute-start.4 = (bf16[512,1280]{1,0:T(8,128)(2,1)}, bf16[512,1280]{1,0:T(8,128)(2,1)}, u32[]{:S(2)}, u32[]{:S(2)}) collective-permute-start(bf16[512,1280]{1,0:T(8,128)(2,1)} %get-tuple-element.84), channel_id=1, source_target_pairs={{0,4},{1,5},{2,6},{3,7},{4,0},{5,1},{6,2},{7,3},{8,12},{9,13},{10,... | collective-permute-start | bytes 3932168 | tf_op jit(solution)/shard_map/ppermute | solution.py:761
  133.3 6.4 %collective-permute-start.5 = (bf16[512,1280]{1,0:T(8,128)(2,1)}, bf16[512,1280]{1,0:T(8,128)(2,1)}, u32[]{:S(2)}, u32[]{:S(2)}) collective-permute-start(bf16[512,1280]{1,0:T(8,128)(2,1)} %get-tuple-element.85), channel_id=1, source_target_pairs={{0,4},{1,5},{2,6},{3,7},{4,0},{5,1},{6,2},{7,3},{8,12},{9,13},{10,... | collective-permute-start | bytes 3932168 | tf_op jit(solution)/shard_map/ppermute | solution.py:761
  133.3 6.7 %collective-permute-start.6 = (bf16[512,1280]{1,0:T(8,128)(2,1)}, bf16[512,1280]{1,0:T(8,128)(2,1)}, u32[]{:S(2)}, u32[]{:S(2)}) collective-permute-start(bf16[512,1280]{1,0:T(8,128)(2,1)} %get-tuple-element.86), channel_id=1, source_target_pairs={{0,4},{1,5},{2,6},{3,7},{4,0},{5,1},{6,2},{7,3},{8,12},{9,13},{10,... | collective-permute-start | bytes 3932168 | tf_op jit(solution)/shard_map/ppermute | solution.py:761
  138.1 31.0 %collective-permute-start.8 = (bf16[3,128,1536]{2,1,0:T(8,128)(2,1)}, bf16[3,128,1536]{2,1,0:T(8,128)(2,1)}, u32[]{:S(2)}, u32[]{:S(2)}) collective-permute-start(bf16[3,128,1536]{2,1,0:T(8,128)(2,1)} %get-tuple-element.88.refs_8_), channel_id=1, source_target_pairs={{0,8},{1,9},{2,10},{3,11},{4,20},{5,21},{6,22},{7,23},{8,0},{9,1},... | collective-permute-start | bytes 3538952 | tf_op jit(solution)/shard_map/ppermute | solution.py:761
  151.2 30.8 %collective-permute-start.9 = (bf16[3,256,1280]{2,1,0:T(8,128)(2,1)}, bf16[3,256,1280]{2,1,0:T(8,128)(2,1)}, u32[]{:S(2)}, u32[]{:S(2)}) collective-permute-start(bf16[3,256,1280]{2,1,0:T(8,128)(2,1)} %get-tuple-element.89.refs_8_), channel_id=1, source_target_pairs={{0,16},{1,17},{2,18},{3,19},{4,5},{5,4},{6,7},{7,6},{8,24},{9,25},... | collective-permute-start | bytes 5898248 | tf_op jit(solution)/shard_map/ppermute | solution.py:761
  181.0 7.4 %collective-permute-start.12 = (bf16[512,1024]{1,0:T(8,128)(2,1)}, bf16[512,1024]{1,0:T(8,128)(2,1)}, u32[]{:S(2)}, u32[]{:S(2)}) collective-permute-start(bf16[512,1024]{1,0:T(8,128)(2,1)} %get-tuple-element.98.refs_5_), channel_id=1, source_target_pairs={{0,4},{1,5},{2,6},{3,7},{4,0},{5,1},{6,2},{7,3},{8,12},{9,13},{10,... | collective-permute-start | bytes 3145736 | tf_op jit(solution)/shard_map/ppermute | solution.py:761
  181.4 8.0 %collective-permute-start.13 = (bf16[512,1024]{1,0:T(8,128)(2,1)}, bf16[512,1024]{1,0:T(8,128)(2,1)}, u32[]{:S(2)}, u32[]{:S(2)}) collective-permute-start(bf16[512,1024]{1,0:T(8,128)(2,1)} %get-tuple-element.99.refs_6_), channel_id=1, source_target_pairs={{0,4},{1,5},{2,6},{3,7},{4,0},{5,1},{6,2},{7,3},{8,12},{9,13},{10,... | collective-permute-start | bytes 3145736 | tf_op jit(solution)/shard_map/ppermute | solution.py:761
  181.5 7.9 %collective-permute-start.14 = (bf16[512,1024]{1,0:T(8,128)(2,1)}, bf16[512,1024]{1,0:T(8,128)(2,1)}, u32[]{:S(2)}, u32[]{:S(2)}) collective-permute-start(bf16[512,1024]{1,0:T(8,128)(2,1)} %get-tuple-element.100.refs_7_), channel_id=1, source_target_pairs={{0,4},{1,5},{2,6},{3,7},{4,0},{5,1},{6,2},{7,3},{8,12},{9,13},{10,... | collective-permute-start | bytes 3145736 | tf_op jit(solution)/shard_map/ppermute | solution.py:761
  181.9 7.5 %collective-permute-start.15 = (bf16[512,1024]{1,0:T(8,128)(2,1)}, bf16[512,1024]{1,0:T(8,128)(2,1)}, u32[]{:S(2)}, u32[]{:S(2)}) collective-permute-start(bf16[512,1024]{1,0:T(8,128)(2,1)} %get-tuple-element.101.refs_8_), channel_id=1, source_target_pairs={{0,4},{1,5},{2,6},{3,7},{4,0},{5,1},{6,2},{7,3},{8,12},{9,13},{10,... | collective-permute-start | bytes 3145736 | tf_op jit(solution)/shard_map/ppermute | solution.py:761
  186.9 20.4 %collective-permute-start.11 = (bf16[3,128,1280]{2,1,0:T(8,128)(2,1)}, bf16[3,128,1280]{2,1,0:T(8,128)(2,1)}, u32[]{:S(2)}, u32[]{:S(2)}) collective-permute-start(bf16[3,128,1280]{2,1,0:T(8,128)(2,1)} %get-tuple-element.105), channel_id=1, source_target_pairs={{0,8},{1,9},{2,10},{3,11},{4,20},{5,21},{6,22},{7,23},{8,0},{9,1},... | collective-permute-start | bytes 2949128 | tf_op jit(solution)/shard_map/ppermute | solution.py:761
  188.4 13.7 %collective-permute-start.10 = (bf16[3,64,1536]{2,1,0:T(8,128)(2,1)}, bf16[3,64,1536]{2,1,0:T(8,128)(2,1)}, u32[]{:S(2)}, u32[]{:S(2)}) collective-permute-start(bf16[3,64,1536]{2,1,0:T(8,128)(2,1)} %get-tuple-element.103.refs_11_), channel_id=1, source_target_pairs={{0,1},{1,0},{2,3},{3,2},{4,12},{5,13},{6,14},{7,15},{8,9},{9,8},{1... | collective-permute-start | bytes 1769480 | tf_op jit(solution)/shard_map/ppermute | solution.py:761
  201.5 33.5 %collective-permute-start.17 = (bf16[1,256,4096]{2,1,0:T(8,128)(2,1)}, bf16[1,256,4096]{2,1,0:T(8,128)(2,1)}, u32[]{:S(2)}, u32[]{:S(2)}) collective-permute-start(bf16[1,256,4096]{2,1,0:T(8,128)(2,1)} %bitcast.46), channel_id=1, source_target_pairs={{0,8},{1,9},{2,10},{3,11},{4,5},{5,4},{6,7},{7,6},{8,0},{9,1},{10,... | collective-permute-start | bytes 6291464 | tf_op jit(solution)/shard_map/ppermute | solution.py:761
  210.7 21.3 %collective-permute-start.18 = (bf16[3,64,1280]{2,1,0:T(8,128)(2,1)}, bf16[3,64,1280]{2,1,0:T(8,128)(2,1)}, u32[]{:S(2)}, u32[]{:S(2)}) collective-permute-start(bf16[3,64,1280]{2,1,0:T(8,128)(2,1)} %get-tuple-element.110), channel_id=1, source_target_pairs={{0,1},{1,0},{2,3},{3,2},{4,12},{5,13},{6,14},{7,15},{8,9},{9,8},{1... | collective-permute-start | bytes 1474568 | tf_op jit(solution)/shard_map/ppermute | solution.py:761
  212.1 19.9 %collective-permute-start.19 = (bf16[3,32,1536]{2,1,0:T(8,128)(2,1)}, bf16[3,32,1536]{2,1,0:T(8,128)(2,1)}, u32[]{:S(2)}, u32[]{:S(2)}) collective-permute-start(bf16[3,32,1536]{2,1,0:T(8,128)(2,1)} %get-tuple-element.107.refs_5_), channel_id=1, source_target_pairs={{0,2},{1,3},{2,0},{3,1},{4,6},{5,7},{6,4},{7,5},{8,10},{9,11},{10,... | collective-permute-start | bytes 884744 | tf_op jit(solution)/shard_map/ppermute | solution.py:761
  219.5 23.8 %collective-permute-start.16 = (bf16[128,1024]{1,0:T(8,128)(2,1)}, bf16[128,1024]{1,0:T(8,128)(2,1)}, u32[]{:S(2)}, u32[]{:S(2)}) collective-permute-start(bf16[128,1024]{1,0:T(8,128)(2,1)} %rim_grad.1.refs_4_), channel_id=1, source_target_pairs={{1,0},{2,1},{3,2},{5,4},{6,5},{7,6},{9,8},{10,9},{11,10},{13,12},{... | collective-permute-start | bytes 786440 | tf_op jit(solution)/shard_map/ppermute | solution.py:999
  239.4 19.4 %collective-permute-start.20 = (bf16[1,128,4096]{2,1,0:T(8,128)(2,1)}, bf16[1,128,4096]{2,1,0:T(8,128)(2,1)}, u32[]{:S(2)}, u32[]{:S(2)}) collective-permute-start(bf16[1,128,4096]{2,1,0:T(8,128)(2,1)} %get-tuple-element.111.refs_6_), channel_id=1, source_target_pairs={{0,16},{1,17},{2,18},{3,19},{4,12},{5,13},{6,14},{7,15},{8,24},{9,... | collective-permute-start | bytes 3145736 | tf_op jit(solution)/shard_map/ppermute | solution.py:761
  240.2 22.5 %collective-permute-start.22 = (bf16[3,32,1280]{2,1,0:T(8,128)(2,1)}, bf16[3,32,1280]{2,1,0:T(8,128)(2,1)}, u32[]{:S(2)}, u32[]{:S(2)}) collective-permute-start(bf16[3,32,1280]{2,1,0:T(8,128)(2,1)} %get-tuple-element.117), channel_id=1, source_target_pairs={{0,2},{1,3},{2,0},{3,1},{4,6},{5,7},{6,4},{7,5},{8,10},{9,11},{10,... | collective-permute-start | bytes 737288 | tf_op jit(solution)/shard_map/ppermute | solution.py:761
  261.8 9.5 %collective-permute-start.21 = (bf16[1,64,4096]{2,1,0:T(8,128)(2,1)}, bf16[1,64,4096]{2,1,0:T(8,128)(2,1)}, u32[]{:S(2)}, u32[]{:S(2)}) collective-permute-start(bf16[1,64,4096]{2,1,0:T(8,128)(2,1)} %get-tuple-element.114.refs_4_), channel_id=1, source_target_pairs={{0,1},{1,0},{2,3},{3,2},{4,20},{5,21},{6,22},{7,23},{8,9},{9,8},{1... | collective-permute-start | bytes 1572872 | tf_op jit(solution)/shard_map/ppermute | solution.py:761
  264.8 14.2 %collective-permute-start.24 = (bf16[3,1,32,2816]{3,2,1,0:T(8,128)(2,1)}, bf16[3,1,32,2816]{3,2,1,0:T(8,128)(2,1)}, u32[]{:S(2)}, u32[]{:S(2)}) collective-permute-start(bf16[3,1,32,2816]{3,2,1,0:T(8,128)(2,1)} %bitcast.47), channel_id=1, source_target_pairs={{0,16},{1,17},{2,18},{3,19},{4,12},{5,13},{6,14},{7,15},{8,24},{9,... | collective-permute-start | bytes 1622024 | tf_op jit(solution)/shard_map/ppermute | solution.py:761
  273.9 10.4 %collective-permute-start.23 = (bf16[1,32,4096]{2,1,0:T(8,128)(2,1)}, bf16[1,32,4096]{2,1,0:T(8,128)(2,1)}, u32[]{:S(2)}, u32[]{:S(2)}) collective-permute-start(bf16[1,32,4096]{2,1,0:T(8,128)(2,1)} %get-tuple-element.119.refs_3_), channel_id=1, source_target_pairs={{0,2},{1,3},{2,0},{3,1},{4,6},{5,7},{6,4},{7,5},{8,10},{9,11},{10,... | collective-permute-start | bytes 786440 | tf_op jit(solution)/shard_map/ppermute | solution.py:761
  281.7 18.3 %collective-permute-start.26 = (bf16[3,2,32,2816]{3,2,1,0:T(8,128)(2,1)}, bf16[3,2,32,2816]{3,2,1,0:T(8,128)(2,1)}, u32[]{:S(2)}, u32[]{:S(2)}) collective-permute-start(bf16[3,2,32,2816]{3,2,1,0:T(8,128)(2,1)} %join.4.refs_2_.refs_1_), channel_id=1, source_target_pairs={{0,8},{1,9},{2,10},{3,11},{4,20},{5,21},{6,22},{7,23},{8,0},{9,1},... | collective-permute-start | bytes 3244040 | tf_op jit(solution)/shard_map/ppermute | solution.py:761
  286.1 20.0 %collective-permute-start.25 = (bf16[1,1,32,4096]{3,2,1,0:T(8,128)(2,1)}, bf16[1,1,32,4096]{3,2,1,0:T(8,128)(2,1)}, u32[]{:S(2)}, u32[]{:S(2)}) collective-permute-start(bf16[1,1,32,4096]{3,2,1,0:T(8,128)(2,1)} %bitcast.50), channel_id=1, source_target_pairs={{0,16},{1,17},{2,18},{3,19},{4,12},{5,13},{6,14},{7,15},{8,24},{9,... | collective-permute-start | bytes 786440 | tf_op jit(solution)/shard_map/ppermute | solution.py:761
  303.3 7.0 %collective-permute-start.28 = (bf16[3,4,32,2816]{3,2,1,0:T(8,128)(2,1)}, bf16[3,4,32,2816]{3,2,1,0:T(8,128)(2,1)}, u32[]{:S(2)}, u32[]{:S(2)}) collective-permute-start(bf16[3,4,32,2816]{3,2,1,0:T(8,128)(2,1)} %join.5.refs_3_.refs_1_), channel_id=1, source_target_pairs={{0,4},{1,5},{2,6},{3,7},{4,0},{5,1},{6,2},{7,3},{8,12},{9,13},{10,... | collective-permute-start | bytes 6488072 | tf_op jit(solution)/shard_map/ppermute | solution.py:761
  308.5 9.7 %collective-permute-start.27 = (bf16[1,2,32,4096]{3,2,1,0:T(8,128)(2,1)}, bf16[1,2,32,4096]{3,2,1,0:T(8,128)(2,1)}, u32[]{:S(2)}, u32[]{:S(2)}) collective-permute-start(bf16[1,2,32,4096]{3,2,1,0:T(8,128)(2,1)} %join.6.refs_5_.refs_1_), channel_id=1, source_target_pairs={{0,8},{1,9},{2,10},{3,11},{4,20},{5,21},{6,22},{7,23},{8,0},{9,1},... | collective-permute-start | bytes 1572872 | tf_op jit(solution)/shard_map/ppermute | solution.py:761
  321.0 3.0 collective-permute-start.29
where the time goes:
time: 333 us; the launch traced here: 329 us
  Pallas kernels  247 us (74%)
  waiting for transfers between devices  45.6 us (14%)
  starting transfers between devices  34.1 us (10%)
    pallas_call x29, Pallas kernels, launch(): pl.pallas_call(body, grid_spec=pltpu.PrefetchScalarGridSpec(num_scalar_pr...  247 us
    ppermute x28, waiting for transfers between devices, swap(): return lax.ppermute(value, ('dp', 'seq'), swap_pairs(n_dp, n_seq, steps))  44.6 us
    ppermute x28, starting transfers between devices, swap(): return lax.ppermute(value, ('dp', 'seq'), swap_pairs(n_dp, n_seq, steps))  26.7 us
    ppermute x2, starting transfers between devices, shifted(): lax.ppermute(value, axis, [(source, source + steps) for source in range(l...  7.41 us
  transfers between devices with their start and end apart: 30, of which 13 were waited for; matrix products, arithmetic and copies ran while one was open for 0% of the time, Pallas kernels for 49%

commit v1 on v0

--- a/solution.py
+++ b/solution.py
@@ -270,7 +270,12 @@
     )
 
 
-def norm_matmul_kernel(facts_ref, x_ref, gain_ref, w_ref, out_ref, normedT_ref, tail_ref, normed_ref, *, slab, put, step, tails):
+def norm_matmul_kernel(facts_ref, x_ref, gain_ref, w_ref, *refs, slab, put, step, beside):
+    if beside:
+        other_ref, out_ref, normedT_ref, otherT_ref, normed_ref = refs
+    else:
+        out_ref, normedT_ref, normed_ref = refs
+
     @pl.when(pl.program_id(0) == 0)
     def _():
         for at in range(0, x_ref.shape[0], step):
@@ -280,55 +285,41 @@
             normed_ref[at : at + step, :] = normed
             store_slabs(normedT_ref, normed.T, facts_ref, put, slab, slice(at, at + step))
 
-        for k, end in enumerate(tails):
-            tail_ref[k * WINDOW : (k + 1) * WINDOW, :] = x_ref[end - WINDOW : end, :]
-
     put_blocks(out_ref, dot(normed_ref[...], w_ref[...]).astype(BF16))
-
-
-def norm_matmul(x, gain, weight, first_column, facts, put, slab, tails, after=()):
+    if beside:
+        store_slabs(otherT_ref, other_ref[...].T, facts_ref, put, slab)
+
+
+def norm_matmul(x, gain, weight, first_column, facts, put, slab, beside=None, after=()):
     tokens, width = x.shape
     columns = weight.shape[1] - first_column
-    tile = 1024
-    skip, wide = first_column // tile, tile // LANES
+    tile = 1024 if beside is None else 768
+    skip, wide, steps = first_column // tile, tile // LANES, columns // tile
+    part = tokens // steps
+    others, turned = [], []
+    if beside is not None:
+        others = [(beside, pl.BlockSpec((part, width), lambda j, *_: (j, 0)))]
+        turned = [((width, tokens), BF16, pl.BlockSpec((width, part), lambda j, *_: (0, j)))]
     return launch(
-        functools.partial(norm_matmul_kernel, slab=slab, put=put, step=min(STEP, tokens), tails=tails),
+        functools.partial(norm_matmul_kernel, slab=slab, put=put, step=min(STEP, tokens), beside=beside is not None),
         "norm_matmul",
-        (columns // tile,),
+        (steps,),
         [facts],
         [
             (x, full(tokens, width)),
             (gain[None], full(1, width)),
             (weight, pl.BlockSpec((width, tile), lambda j, *_: (0, skip + j))),
-        ],
+        ]
+        + others,
         [
             ((columns // LANES, tokens, LANES), BF16, pl.BlockSpec((wide, tokens, LANES), lambda j, *_: (j, 0, 0))),
             ((width, tokens), BF16, full(width, tokens)),
-            ((len(tails) * WINDOW, width), BF16, full(len(tails) * WINDOW, width)),
-        ],
+        ]
+        + turned,
         [pltpu.VMEM((tokens, width), BF16)],
         us=8,
         after=after,
     )
-
-
-def turn_kernel(facts_ref, x_ref, out_ref, *, slab, put):
-    store_slabs(out_ref, x_ref[...].T, facts_ref, put, slab)
-
-
-def turn(x, facts, put, slab, after=()):
-    tokens, width = x.shape
-    step = 2 * STEP
-    return launch(
-        functools.partial(turn_kernel, slab=slab, put=put),
-        "turn",
-        (tokens // step,),
-        [facts],
-        [(x, pl.BlockSpec((step, width), lambda m, *_: (m, 0)))],
-        [((width, tokens), BF16, pl.BlockSpec((width, step), lambda m, *_: (0, m)))],
-        us=8,
-        after=after,
-    )[0]
 
 
 def out_proj_kernel(facts_ref, att_ref, w_ref, x_ref, gain_ref, resid_ref, normed_ref, normedT_ref, *, slab, put):
@@ -528,7 +519,7 @@
     out_ref[...] = total.astype(BF16)
 
 
-def ff_out(hiddens, w_down, resid, after=()):
+def ff_out(hiddens, w_down, resid, us, after=()):
     tokens, width = resid.shape
     rows = lambda columns: pl.BlockSpec((STEP, columns), lambda m: (m, 0))
     return launch(
@@ -539,7 +530,7 @@
         [(hidden, rows(hidden.shape[1])) for hidden in hiddens]
         + [(w_down.T, full(FF, width)), (resid, rows(width))],
         [((tokens, width), BF16, rows(width))],
-        us=1,
+        us=us,
         after=after,
     )[0]
 
@@ -549,34 +540,31 @@
     attT_ref, oneT_ref, rimT_ref, drb_ref, dqkv_ref, drim_ref = refs[:6]
     kind = pl.program_id(0)
 
-    def put(total, index):
+    def put(total):
         if split:
-            got_ref = refs[6 + index]
-            send_ref, keep_ref = refs[-2:]
+            got_ref, send_ref, keep_ref = refs[-3:]
             part = send_ref.shape[0]
             own = facts_ref[bit]
             for out_ref, half in ((send_ref, 1 - own), (keep_ref, own)):
                 rows = pl.ds(pl.multiple_of(half * part, part), part)
                 out_ref[...] = (total(rows) + got_ref[rows, :].astype(F32)).astype(BF16)
         else:
-            refs[6 + index][...] = total(slice(None)).astype(BF16)
+            refs[-1][...] = total(slice(None)).astype(BF16)
 
     @pl.when(kind == 0)
     def _():
         right = side_by_side(drb_ref)
-        put(lambda rows: dot(attT_ref[rows, :], right), 0)
+        put(lambda rows: dot(attT_ref[rows, :], right))
 
     @pl.when(kind == 1)
     def _():
         right = side_by_side(dqkv_ref)
-        put(lambda rows: dot(oneT_ref[rows, :], right), 1)
-
-    for index in (2, 3):
-
-        @pl.when(kind == index)
-        def _():
-            right, rim = side_by_side(dqkv_ref), side_by_side(drim_ref)
-            put(lambda rows: dot(oneT_ref[rows, :], right) + dot(rimT_ref[rows, :], rim), index)
+        put(lambda rows: dot(oneT_ref[rows, :], right))
+
+    @pl.when(kind > 1)
+    def _():
+        right, rim = side_by_side(dqkv_ref), side_by_side(drim_ref)
+        put(lambda rows: dot(oneT_ref[rows, :], right) + dot(rimT_ref[rows, :], rim))
 
 
 def att_grad(facts, att_turned, one_turned, rim_turned, drb, dqkv, drim, bit=None, got=None, us=8, after=()):
@@ -595,13 +583,13 @@
         (drim, pl.BlockSpec((None, blocks, rim, LANES), lambda j, *_: (jnp.maximum(j - 2, 0), 0, 0, 0))),
     ]
     columns = 4 * width
-    parts = [full(width // 2, width)] * 4
+    tile = pl.BlockSpec((width // 2, width), lambda j, *_: (0, j))
     if split:
-        inputs += list(zip(got, parts))
+        inputs.append((got, tile))
         part = ((width // 4, columns), BF16, pl.BlockSpec((width // 4, width), lambda j, *_: (0, j)))
         outputs = [part, part]
     else:
-        outputs = [((width // 2, width), BF16, spec) for spec in parts]
+        outputs = [((width // 2, columns), BF16, tile)]
     return launch(
         functools.partial(att_grad_kernel, bit=bit),
         "att_grad",
@@ -614,49 +602,38 @@
     )
 
 
-def input_grad_kernel(dqkv_ref, w_ref, x_ref, gain_ref, drb_ref, back_ref, out_ref, acc_ref, *, rows, group):
-    k = pl.program_id(0)
-    tokens = acc_ref.shape[0]
-    part = dot(side_by_side(dqkv_ref), w_ref[...], 1, 1)
-
-    @pl.when(k == 0)
-    def _():
-        acc_ref[...] = part
-
-    @pl.when(k > 0)
-    def _():
-        acc_ref[...] += part
-
-    @pl.when(k == 2)
-    def _():
-        for at in range(0, tokens, STEP):
-            here = slice(at, at + STEP)
-            grad = norm_back(acc_ref[here, :], x_ref[here, :].astype(F32), gain_ref[...])
-            out_ref[here, :] = grad + side_by_side(drb_ref.at[:, here, :]).astype(F32)
-        for row in range(rows):
-            tail = slice((row + 1) * group - WINDOW, (row + 1) * group)
-            out_ref[tail, :] += back_ref[row * WINDOW : (row + 1) * WINDOW, :].astype(F32)
-
-
-def input_grad(dqkv, w_qkv, x, gain, drb, back, rows, group, after=()):
+def input_grad_kernel(dqkv_ref, w_ref, x_ref, gain_ref, drb_ref, back_ref, out_ref, *, tails):
+    step = out_ref.shape[0]
+    grads = jnp.concatenate([side_by_side(dqkv_ref.at[kind]) for kind in range(3)], axis=1)
+    grad = norm_back(dot(grads, w_ref[...], 1, 1), x_ref[...].astype(F32), gain_ref[...])
+    out_ref[...] = grad + side_by_side(drb_ref).astype(F32)
+    for row, end in enumerate(tails):
+        block, last = divmod(end - WINDOW, step)
+
+        @pl.when(pl.program_id(0) == block)
+        def _():
+            out_ref[last : last + WINDOW, :] += back_ref[row * WINDOW : (row + 1) * WINDOW, :].astype(F32)
+
+
+def input_grad(dqkv, w_qkv, x, gain, drb, back, tails, us, after=()):
     tokens, width = x.shape
-    whole = full(tokens, width)
+    blocks = width // LANES
+    rows = pl.BlockSpec((STEP, width), lambda m: (m, 0))
     return launch(
-        functools.partial(input_grad_kernel, rows=rows, group=group),
+        functools.partial(input_grad_kernel, tails=tails),
         "input_grad",
-        (3,),
+        (tokens // STEP,),
         [],
         [
-            (dqkv, pl.BlockSpec((None, width // LANES, tokens, LANES), lambda j: (j, 0, 0, 0))),
-            (w_qkv, pl.BlockSpec((width, width), lambda j: (0, j))),
-            (x, whole),
+            (dqkv, pl.BlockSpec((3, blocks, STEP, LANES), lambda m: (0, 0, m, 0))),
+            (w_qkv, full(*w_qkv.shape)),
+            (x, rows),
             (gain[None], full(1, width)),
-            (drb, full(*drb.shape)),
-            (back, full(rows * WINDOW, width)),
+            (drb, pl.BlockSpec((blocks, STEP, LANES), lambda m: (0, m, 0))),
+            (back, full(*back.shape)),
         ],
-        [((tokens, width), F32, whole)],
-        [pltpu.VMEM((tokens, width), F32)],
-        us=8,
+        [((tokens, width), F32, rows)],
+        us=us,
         after=after,
     )[0]
 
@@ -697,7 +674,7 @@
             out_ref[...] = (keep_ref[:, index].astype(F32) + got_ref[:, index].astype(F32)).astype(BF16)
 
 
-def add_and_cut(facts, items, after=()):
+def add_and_cut(facts, items, us, after=()):
     inputs, outputs = [], []
     for keep, got, _ in items:
         kinds, rows, columns = keep.shape
@@ -707,8 +684,31 @@
         part = pl.BlockSpec((kinds, rows // 2, columns // 2), lambda j, *_: (0, 0, j))
         outputs += [((kinds, rows // 2, columns), BF16, part)] * 2
     kernel = functools.partial(add_kernel, bits=[bit for _, _, bit in items])
-    parts = launch(kernel, "add_and_cut", (2,), [facts], inputs, outputs, us=8, after=after)
+    parts = launch(kernel, "add_and_cut", (2,), [facts], inputs, outputs, us=us, after=after)
     return [(parts[2 * k], parts[2 * k + 1]) for k in range(len(items))]
+
+
+def merge_kernel(facts_ref, *refs, bit):
+    *parts, send_ref, keep_ref = refs
+    for out_ref, index in ((send_ref, 1 - facts_ref[bit]), (keep_ref, facts_ref[bit])):
+        first = 0
+        for keep, got in zip(parts[::2], parts[1::2]):
+            columns = keep.shape[3]
+            total = keep[:, index].astype(F32) + got[:, index].astype(F32)
+            out_ref[:, :, first : first + columns] = total.astype(BF16)
+            first += columns
+
+
+def merge_and_cut(facts, pieces, bit, us, after=()):
+    inputs = []
+    for keep, got in pieces:
+        kinds, rows, columns = keep.shape
+        spec = pl.BlockSpec((1, 2, rows // 2, columns), lambda j, *_: (j, 0, 0, 0))
+        inputs += [(value.reshape(kinds, 2, rows // 2, columns), spec) for value in (keep, got)]
+    columns = sum(keep.shape[2] for keep, _ in pieces)
+    part = ((kinds, rows // 2, columns), BF16, pl.BlockSpec((1, rows // 2, columns), lambda j, *_: (j, 0, 0)))
+    kernel = functools.partial(merge_kernel, bit=bit)
+    return launch(kernel, "merge_and_cut", (kinds,), [facts], inputs, [part, part], us=us, after=after)
 
 
 def log2(count):
@@ -821,11 +821,19 @@
         return self.done == len(self.stages)
 
 
-def advance(facts, *chunks, after=()):
-    parts = add_and_cut(facts, [(chunk.keep, chunk.got, chunk.bit()) for chunk in chunks], after=after)
+def advance(facts, *chunks, us=8, after=()):
+    parts = add_and_cut(facts, [(chunk.keep, chunk.got, chunk.bit()) for chunk in chunks], us, after)
     for chunk, (send, keep) in zip(chunks, parts):
         chunk.go(send, keep)
     return parts[0][0]
+
+
+def merge(facts, *chunks, us, after=()):
+    whole = Chunk(chunks[0].flavour)
+    whole.done = chunks[0].done
+    pieces = [(chunk.keep, chunk.got) for chunk in chunks]
+    whole.go(*merge_and_cut(facts, pieces, whole.bit(), us, after))
+    return whole
 
 
 def finish_kernel(*refs):
@@ -1025,15 +1033,12 @@
     dy = cotangent.reshape(tokens, width)
 
     tails = [(row + 1) * group for row in range(rows)]
-    qkv, one_turned, x_tail = norm_matmul(x, gain_attn, w_qkv, 0, facts, put[0], slab, tails)
-    x_rim = shifted(x_tail, "seq", 1)
-    dy_turned = turn(dy, facts, put[1], slab, after=[qkv])
-    kv_rim, rim_turned, _ = norm_matmul(
-        x_rim, gain_attn, w_qkv, width, facts, put[0], slab, [WINDOW], after=[dy_turned]
-    )
-    att, att_turned = attend(qkv, kv_rim, doc_start, facts, put[0], slab)
+    x_rim = shifted(inputs[:, group - WINDOW :], "seq", 1).reshape(rows * WINDOW, width)
+    qkv, one_turned, dy_turned = norm_matmul(x, gain_attn, w_qkv, 0, facts, put[1], slab, dy)
+    kv_rim, rim_turned = norm_matmul(x_rim, gain_attn, w_qkv, width, facts, put[1], slab, after=[qkv])
+    att, att_turned = attend(qkv, kv_rim, doc_start, facts, put[1], slab)
     resid, normed_two, two_turned = out_proj(att, w_out, x, gain_mlp, facts, put[1], slab)
-    one_turned, rim_turned, att_turned = [in_order(turned, 0) for turned in (one_turned, rim_turned, att_turned)]
+    one_turned, rim_turned, att_turned = [in_order(turned, 1) for turned in (one_turned, rim_turned, att_turned)]
     two_turned, dy_turned = [in_order(turned, 1) for turned in (two_turned, dy_turned)]
 
     def feed(first, count, total=None, end=None, after=()):
@@ -1056,22 +1061,22 @@
     token = advance(facts, one, after=[da])
     token = keep_ff(two, hidden_two, dgu_two, after=[token])
     dqkv, drim = attend_back(qkv, kv_rim, doc_start, facts, da, after=[token])
-    att = Chunk(0)
+    att = Chunk(1)
     grads = (facts, att_turned, one_turned, rim_turned, drb, dqkv, drim)
-    sends = att_grad(*grads, after=[one.got])
-    att.between_cores(*sends)
-    token = advance(facts, one, two, after=sends)
-    send, keep = att_grad(*grads, att.bit(), att.got, after=[token])
-    att.go(send[None], keep[None])
-    token = advance(facts, one, two, after=[send])
+    (send,) = att_grad(*grads, after=[one.got])
+    att.between_cores(send)
+    token = advance(facts, one, two, us=30, after=[send])
     back = rim_grad(drim, w_qkv, x_rim, gain_attn, after=[token])
     back_got = shifted(back, "seq", -1)
-    outputs = ff_out([hidden_one, hidden_two], w_down, resid, after=[back])
-    token = advance(facts, att, two, after=[outputs, one.got])
+    send, keep = att_grad(*grads, att.bit(), att.got[0], after=[back])
+    att.go(send[None], keep[None])
+    token = advance(facts, one, two, after=[send, back_got])
+    grad_inputs = input_grad(dqkv, w_qkv, x, gain_attn, drb, back_got, tails, us=15, after=[token])
+    token = advance(facts, att, two, after=[grad_inputs, one.got])
     while not (one.last and two.last):
         token = advance(facts, *(chunk for chunk in (one, two) if not chunk.last), after=[token])
-    grad_inputs = input_grad(dqkv, w_qkv, x, gain_attn, drb, back_got, rows, group, after=[token])
-    token = advance(facts, att, after=[grad_inputs])
+    outputs = ff_out([hidden_one, hidden_two], w_down, resid, us=8, after=[token])
+    token = advance(facts, att, after=[outputs])
     gather_ff = Gather(facts, finish(one, two, after=[token]))
     token = gather_ff.value
     while not att.last:
@@ -1079,12 +1084,12 @@
     token = gather_ff.step(after=[token])
     gather = Gather(facts, finish(att, after=[token]))
     if ordered and n_dp == 8:
-        token = gather_ff.step(after=[gather.value])
+        token = gather.step(us=1, after=[gather.value])
+        token = gather_ff.step(after=[token])
         token = gather.step(us=24, after=[token])
         total_gate_up, turned_down, gain_two = put_ff(gather_ff, w_gate_up, gain_mlp, after=[token])
         total_down = turned_down.T
-        gather.step(after=[total_gate_up])
-        total_qkv, total_out, gain_one = put_att(gather, w_qkv, gain_attn)
+        total_qkv, total_out, gain_one = put_att(gather, w_qkv, gain_attn, after=[total_gate_up])
         gain_one, gain_two = gain_one[0], gain_two[0]
     else:
         for both in (gather_ff, gather):

time: 333 us -> 342 us (1.027)
  the two profiles are of different devices: /device:TPU:0 before, /device:TPU:9 now
where the time goes in v1:
time: 342 us; the launch traced here: 337 us
  Pallas kernels  252 us (74%)
  waiting for transfers between devices  64 us (19%)
  starting transfers between devices  17.8 us (5%)
    pallas_call x28, Pallas kernels, launch(): pl.pallas_call(body, grid_spec=pltpu.PrefetchScalarGridSpec(num_scalar_pr...  252 us
    ppermute x25, waiting for transfers between devices, swap(): return lax.ppermute(value, ('dp', 'seq'), swap_pairs(n_dp, n_seq, steps))  64 us
    ppermute x25, starting transfers between devices, swap(): return lax.ppermute(value, ('dp', 'seq'), swap_pairs(n_dp, n_seq, steps))  11.9 us
  transfers between devices with their start and end apart: 27, of which 11 were waited for; matrix products, arithmetic and copies ran while one was open for 0% of the time, Pallas kernels for 52%

profile of v1, /device:TPU:9, one launch (start us, length us, event | category | flops | bytes accessed | tf_op | source)
XLA Modules:
  0.0 337.3 jit_solution(4951102710848572487)
XLA Ops:
  0.6 1.7 slice.3
  2.3 3.2 collective-permute-start
  5.5 1.2 dynamic-slice_bitcast_fusion.refs_0_
  6.7 14.0 %norm_matmul.2 = (bf16[24,1024,128]{2,1,0:T(8,128)(2,1)}, bf16[1024,1024]{1,0:T(8,128)(2,1)}, bf16[1024,1024]{1,0:T(8,128)(2,1)}) custom-call(s32[78]{0:T(128)} %dynamic-slice_bitcast_fusion.refs_0_, bf16[1024,1024]{1,0:T(8,128)(2,1)} %bitcast.40, f32[1,1024]{1,0:T(1,128)} %bitcast.53, bf16[1024,3072]{1,0:T(8,128)(2,1)} %refs_3_.7, bf16[1024,1024]{1,0:T(8,128)(2,1)} %bitcast.37), custom_call_target="tpu_custom_call" | custom-call | flops 8800000000 | bytes 209756 | tf_op jit(solution)/shard_map/norm_matmul/pallas_call | solution.py:46
  20.7 4.2 %norm_matmul.3 = (bf16[16,128,128]{2,1,0:T(8,128)(2,1)}, bf16[1024,128]{1,0:T(8,128)(2,1)}) custom-call(s32[78]{0:T(128)} %dynamic-slice_bitcast_fusion.refs_0_, bf16[128,1024]{1,0:T(8,128)(2,1)} %bitcast.4.refs_1_.refs_3_, f32[1,1024]{1,0:T(1,128)} %bitcast.54, bf16[1024,3072]{1,0:T(8,128)(2,1)} %refs_3_.7, ...), custom_call_target="tpu_custom_call" | custom-call | flops 8800000000 | bytes 73441 | tf_op jit(solution)/shard_map/norm_matmul/pallas_call | solution.py:46
  24.9 10.6 %attend.1 = (bf16[8,1024,128]{2,1,0:T(8,128)(2,1)}, bf16[1024,1024]{1,0:T(8,128)(2,1)}) custom-call(s32[78]{0:T(128)} %dynamic-slice_bitcast_fusion.refs_0_, s32[2,512]{1,0:T(2,128)} %refs_1_.5, bf16[24,1024,128]{2,1,0:T(8,128)(2,1)} %get-tuple-element.63.refs_4_.refs_2_.refs_3_, bf16[24,1024,128]{2,1,0:T(8,128)(2,1)} %get-tuple-element.63.refs_4_.refs_2_.refs_3_, ...), custom_call_target="tpu_custom_call" | custom-call | flops 8800000000 | bytes 241213 | tf_op jit(solution)/shard_map/attend/pallas_call | solution.py:46
  35.5 8.0 %out_proj.1 = (bf16[1024,1024]{1,0:T(8,128)(2,1)}, bf16[1024,1024]{1,0:T(8,128)(2,1)}, bf16[1024,1024]{1,0:T(8,128)(2,1)}) custom-call(s32[78]{0:T(128)} %dynamic-slice_bitcast_fusion.refs_0_, bf16[8,1024,128]{2,1,0:T(8,128)(2,1)} %get-tuple-element.65.refs_1_, bf16[1024,1024]{1,0:T(8,128)(2,1)} %refs_12_.1, bf16[1024,1024]{1,0:T(8,128)(2,1)} %bitcast.41, ...), custom_call_target="tpu_custom_call" | custom-call | flops 8800000000 | bytes 125870 | tf_op jit(solution)/shard_map/out_proj/pallas_call | solution.py:46
  43.4 30.2 %feed_forward.2 = (bf16[1024,1536]{1,0:T(8,128)(2,1)}, bf16[2,1024,1536]{2,1,0:T(8,128)(2,1)}, bf16[512,1536]{1,0:T(8,128)(2,1)}, bf16[512,1536]{1,0:T(8,128)(2,...) custom-call(bf16[1024,1024]{1,0:T(8,128)(2,1)} %get-tuple-element.66.refs_0_, bf16[1024,1024]{1,0:T(8,128)(2,1)} %bitcast.38, ...), custom_call_target="tpu_custom_call" | custom-call | flops 8800000000 | bytes 774635 | tf_op jit(solution)/shard_map/feed_forward/pallas_call | solution.py:46
  73.7 1.0 collective-permute-start.1
  74.7 0.1 collective-permute-start.2
  74.8 0.4 collective-permute-start.3
  75.2 2.9 collective-permute-done.1.refs_5_
  78.1 2.2 collective-permute-done.2.refs_6_
  80.3 2.2 collective-permute-done.3.refs_7_
  82.6 12.3 %ff_grad.2 = (bf16[3,256,1536]{2,1,0:T(8,128)(2,1)}, bf16[3,256,1536]{2,1,0:T(8,128)(2,1)}) custom-call(s32[78]{0:T(128)} %dynamic-slice_bitcast_fusion.refs_0_, bf16[1024,1024]{1,0:T(8,128)(2,1)} %get-tuple-element.67.refs_2_.refs_1_, bf16[1024,1024]{1,0:T(8,128)(2,1)} %get-tuple-element.68.refs_3_.refs_2_, ...), custom_call_target="tpu_custom_call" | custom-call | flops 8800000000 | bytes 230686 | tf_op jit(solution)/shard_map/ff_grad/pallas_call | solution.py:46
  94.9 0.9 collective-permute-start.7
  95.9 32.0 %feed_forward.3 = (bf16[1024,1280]{1,0:T(8,128)(2,1)}, bf16[2,1024,1280]{2,1,0:T(8,128)(2,1)}, bf16[512,1280]{1,0:T(8,128)(2,1)}, bf16[512,1280]{1,0:T(8,128)(2,...) custom-call(bf16[1024,1024]{1,0:T(8,128)(2,1)} %get-tuple-element.66.refs_0_, ...), custom_call_target="tpu_custom_call" | custom-call | flops 8800000000 | bytes 834969 | tf_op jit(solution)/shard_map/feed_forward/pallas_call | solution.py:46
  127.8 1.1 collective-permute-start.4
  128.9 0.1 collective-permute-start.5
  129.0 0.4 collective-permute-start.6
  129.4 0.0 collective-permute-done.7
  129.4 4.3 %add_and_cut.6 = (bf16[3,128,1536]{2,1,0:T(8,128)(2,1)}, bf16[3,128,1536]{2,1,0:T(8,128)(2,1)}) custom-call(s32[78]{0:T(128)} %dynamic-slice_bitcast_fusion.refs_0_, bf16[3,2,128,1536]{3,2,1,0:T(8,128)(2,1)} %bitcast.60, bf16[3,2,128,1536]{3,2,1,0:T(8,128)(2,1)} %bitcast.8.refs_2_, bf16[8,1024,128]{2,1,0:T(8,128)(2,1)} %get-tuple-element.82.refs_3_.refs_7_), custom_call_target="tpu_custom_call" | custom-call | flops 8800000000 | bytes 70778 | tf_op jit(solution)/shard_map/add_and_cut/pallas_call | solution.py:46
  133.8 0.3 collective-permute-start.8
  134.1 0.0 collective-permute-done.4.refs_5_
  134.1 0.0 collective-permute-done.5.refs_6_
  134.1 1.6 collective-permute-done.6.refs_7_
  135.7 11.2 %ff_grad.3 = (bf16[3,256,1280]{2,1,0:T(8,128)(2,1)}, bf16[3,256,1280]{2,1,0:T(8,128)(2,1)}) custom-call(s32[78]{0:T(128)} %dynamic-slice_bitcast_fusion.refs_0_, bf16[1024,1024]{1,0:T(8,128)(2,1)} %get-tuple-element.67.refs_2_.refs_1_, bf16[1024,1024]{1,0:T(8,128)(2,1)} %get-tuple-element.68.refs_3_.refs_2_, ...), custom_call_target="tpu_custom_call" | custom-call | flops 8800000000 | bytes 199229 | tf_op jit(solution)/shard_map/ff_grad/pallas_call | solution.py:46
  146.9 0.9 collective-permute-start.10
  147.7 16.4 %attend_back.1 = (bf16[3,8,1024,128]{3,2,1,0:T(8,128)(2,1)}, bf16[2,8,128,128]{3,2,1,0:T(8,128)(2,1)}) custom-call(s32[78]{0:T(128)} %dynamic-slice_bitcast_fusion.refs_0_, s32[2,512]{1,0:T(2,128)} %refs_1_.5, bf16[24,1024,128]{2,1,0:T(8,128)(2,1)} %get-tuple-element.63.refs_4_.refs_2_.refs_3_, ...), custom_call_target="tpu_custom_call" | custom-call | flops 8800000000 | bytes 288399 | tf_op jit(solution)/shard_map/attend_back/pallas_call | solution.py:46
  164.2 0.0 collective-permute-done.8.refs_7_
  164.2 21.6 %att_grad.2.refs_5_ = bf16[512,4096]{1,0:T(8,128)(2,1)} custom-call(s32[78]{0:T(128)} %dynamic-slice_bitcast_fusion.refs_0_, bf16[1024,1024]{1,0:T(8,128)(2,1)} %get-tuple-element.78.refs_1_, bf16[1024,1024]{1,0:T(8,128)(2,1)} %get-tuple-element.79.refs_2_, bf16[1024,128]{1,0:T(8,128)(2,1)} %get-tuple-element.80.refs_3_, ...), custom_call_target="tpu_custom_call" | custom-call | flops 8800000000 | bytes 175636 | tf_op jit(solution)/shard_map/att_grad/pallas_call | solution.py:46
  185.8 0.1 collective-permute-start.9
  185.9 4.9 %add_and_cut.7 = (bf16[3,64,1536]{2,1,0:T(8,128)(2,1)}, bf16[3,64,1536]{2,1,0:T(8,128)(2,1)}, bf16[3,128,1280]{2,1,0:T(8,128)(2,1)}, bf16[3,128,1280]{2,1,0:T(8,128)(2,1)}) custom-call(s32[78]{0:T(128)} %dynamic-slice_bitcast_fusion.refs_0_, bf16[3,2,64,1536]{3,2,1,0:T(8,128)(2,1)} %bitcast.64, bf16[3,2,64,1536]{3,2,1,0:T(8,128)(2,1)} %bitcast.10.refs_2_, ...), custom_call_target="tpu_custom_call" | custom-call | flops 32999999488 | bytes 94371 | tf_op jit(solution)/shard_map/add_and_cut/pallas_call | solution.py:46
  190.8 1.1 collective-permute-start.13
  191.9 4.8 %rim_grad.1.refs_8_ = bf16[128,1024]{1,0:T(8,128)(2,1)} custom-call(bf16[2,8,128,128]{3,2,1,0:T(8,128)(2,1)} %get-tuple-element.91.refs_6_.refs_0_, bf16[1024,3072]{1,0:T(8,128)(2,1)} %refs_3_.7, bf16[1024,3072]{1,0:T(8,128)(2,1)} %refs_3_.7, bf16[128,1024]{1,0:T(8,128)(2,1)} %bitcast.4.refs_1_.refs_3_, f32[1,1024]{1,0:T(1,128)} %bitcast.55, ...), custom_call_target="tpu_custom_call" | custom-call | flops 8800000000 | bytes 136355 | tf_op jit(solution)/shard_map/rim_grad/pallas_call | solution.py:46
  196.7 1.2 collective-permute-start.12
  197.9 2.8 collective-permute-start.14
  200.7 11.6 %att_grad.3 = (bf16[256,4096]{1,0:T(8,128)(2,1)}, bf16[256,4096]{1,0:T(8,128)(2,1)}) custom-call(s32[78]{0:T(128)} %dynamic-slice_bitcast_fusion.refs_0_, bf16[1024,1024]{1,0:T(8,128)(2,1)} %get-tuple-element.78.refs_1_, bf16[1024,1024]{1,0:T(8,128)(2,1)} %get-tuple-element.79.refs_2_, bf16[1024,128]{1,0:T(8,128)(2,1)} %get-tuple-element.80.refs_3_, ...), custom_call_target="tpu_custom_call" | custom-call | flops 8800000000 | bytes 217579 | tf_op jit(solution)/shard_map/att_grad/pallas_call | solution.py:46
  212.3 3.5 %add_and_cut.8 = (bf16[3,32,1536]{2,1,0:T(8,128)(2,1)}, bf16[3,32,1536]{2,1,0:T(8,128)(2,1)}, bf16[3,64,1280]{2,1,0:T(8,128)(2,1)}, bf16[3,64,1280]{2,1,0:T(8,128)(2,1)}) custom-call(s32[78]{0:T(128)} %dynamic-slice_bitcast_fusion.refs_0_, bf16[3,2,32,1536]{3,2,1,0:T(8,128)(2,1)} %bitcast.67, bf16[3,2,32,1536]{3,2,1,0:T(8,128)(2,1)} %bitcast.17.refs_2_, ...), custom_call_target="tpu_custom_call" | custom-call | flops 8800000000 | bytes 47185 | tf_op jit(solution)/shard_map/add_and_cut/pallas_call | solution.py:46
  215.8 0.3 collective-permute-start.15
  216.1 2.3 collective-permute-start.16
  218.4 13.0 %input_grad.1.refs_5_ = f32[1024,1024]{1,0:T(8,128)} custom-call(bf16[3,8,1024,128]{3,2,1,0:T(8,128)(2,1)} %get-tuple-element.90.refs_5_.refs_0_, bf16[1024,3072]{1,0:T(8,128)(2,1)} %refs_3_.7, bf16[1024,1024]{1,0:T(8,128)(2,1)} %bitcast.42, f32[1,1024]{1,0:T(1,128)} %bitcast.56, bf16[8,1024,128]{2,1,0:T(8,128)(2,1)} %get-tuple-element.81.refs_4_, ...), custom_call_target="tpu_custom_call" | custom-call | flops 16499999744 | bytes 212377 | tf_op jit(solution)/shard_map/input_grad/pallas_call | solution.py:46
  231.4 20.4 %collective-permute-done.16.refs_6_.refs_1_ = bf16[3,32,1536]{2,1,0:T(8,128)(2,1)} collective-permute-done((bf16[3,32,1536]{2,1,0:T(8,128)(2,1)}, bf16[3,32,1536]{2,1,0:T(8,128)(2,1)}, u32[]{:S(2)}, u32[]{:S(2)}) %collective-permute-start.16) | collective-permute-done | bytes 294944 | tf_op jit(solution)/shard_map/ppermute | solution.py:761
  251.8 4.4 %add_and_cut.9 = (bf16[1,128,4096]{2,1,0:T(8,128)(2,1)}, bf16[1,128,4096]{2,1,0:T(8,128)(2,1)}, bf16[3,32,1280]{2,1,0:T(8,128)(2,1)}, bf16[3,32,1280]{2,1,0:T(8,128)(2,1)}) custom-call(s32[78]{0:T(128)} %dynamic-slice_bitcast_fusion.refs_0_, bf16[1,2,128,4096]{3,2,1,0:T(8,128)(2,1)} %bitcast.62, bf16[1,2,128,4096]{3,2,1,0:T(8,128)(2,1)} %bitcast.15.refs_2_, ...), custom_call_target="tpu_custom_call" | custom-call | flops 8800000000 | bytes 77660 | tf_op jit(solution)/shard_map/add_and_cut/pallas_call | solution.py:46
  256.2 0.0 collective-permute-start.17
  256.2 0.1 collective-permute-start.19
  256.4 10.9 %ff_out.1.refs_3_ = bf16[1024,1024]{1,0:T(8,128)(2,1)} custom-call(bf16[1024,1536]{1,0:T(8,128)(2,1)} %get-tuple-element.69.refs_3_.refs_0_, bf16[1024,1280]{1,0:T(8,128)(2,1)} %get-tuple-element.77.refs_3_.refs_1_, bf16[2752,1024]{1,0:T(8,128)(2,1)} %bitcast.36, bf16[1024,1024]{1,0:T(8,128)(2,1)} %get-tuple-element.71.refs_10_.refs_3_, ...), custom_call_target="tpu_custom_call" | custom-call | flops 8800000000 | bytes 155975 | tf_op jit(solution)/shard_map/ff_out/pallas_call | solution.py:46
  267.3 6.1 %collective-permute-done.17 = bf16[1,128,4096]{2,1,0:T(8,128)(2,1)} collective-permute-done((bf16[1,128,4096]{2,1,0:T(8,128)(2,1)}, bf16[1,128,4096]{2,1,0:T(8,128)(2,1)}, u32[]{:S(2)}, u32[]{:S(2)}) %collective-permute-start.17) | collective-permute-done | bytes 1048608 | tf_op jit(solution)/shard_map/ppermute | solution.py:761
  273.4 3.0 add_and_cut.10
  276.4 2.1 finish.2
  278.6 1.5 collective-permute-start.21
  280.0 7.2 %collective-permute-done.18 = bf16[1,64,4096]{2,1,0:T(8,128)(2,1)} collective-permute-done((bf16[1,64,4096]{2,1,0:T(8,128)(2,1)}, bf16[1,64,4096]{2,1,0:T(8,128)(2,1)}, u32[]{:S(2)}, u32[]{:S(2)}) %collective-permute-start.18) | collective-permute-done | bytes 524320 | tf_op jit(solution)/shard_map/ppermute | solution.py:761
  287.2 2.6 add_and_cut.11
  289.8 9.0 %collective-permute-done.21.refs_2_ = bf16[3,1,32,2816]{3,2,1,0:T(8,128)(2,1)} collective-permute-done((bf16[3,1,32,2816]{3,2,1,0:T(8,128)(2,1)}, bf16[3,1,32,2816]{3,2,1,0:T(8,128)(2,1)}, u32[]{:S(2)}, u32[]{:S(2)}) %collective-permute-start.21) | collective-permute-done | bytes 540704 | tf_op jit(solution)/shard_map/ppermute | solution.py:761
  298.8 2.7 join.4.refs_2_.refs_1_
  301.5 1.8 finish.3
  303.3 7.3 %collective-permute-done.22.refs_2_ = bf16[1,1,32,4096]{3,2,1,0:T(8,128)(2,1)} collective-permute-done((bf16[1,1,32,4096]{3,2,1,0:T(8,128)(2,1)}, bf16[1,1,32,4096]{3,2,1,0:T(8,128)(2,1)}, u32[]{:S(2)}, u32[]{:S(2)}) %collective-permute-start.22) | collective-permute-done | bytes 262176 | tf_op jit(solution)/shard_map/ppermute | solution.py:761
  310.6 2.5 join.5.refs_3_.refs_1_
  313.1 2.7 collective-permute-done.24.refs_2_
  315.8 3.3 join.6.refs_3_.refs_1_
  319.1 2.3 collective-permute-done.23.refs_2_
  321.4 2.7 join.7.refs_5_.refs_1_
  324.2 8.0 %put_ff.1 = (f32[256,5504]{1,0:T(8,128)}, f32[2752,256]{1,0:T(8,128)}, f32[1,256]{1,0:T(1,128)}) custom-call(s32[78]{0:T(128)} %dynamic-slice_bitcast_fusion.refs_0_, bf16[3,4,32,2816]{3,2,1,0:T(8,128)(2,1)} %join.6.refs_3_.refs_1_, bf16[3,4,32,2816]{3,2,1,0:T(8,128)(2,1)} %collective-permute-done.26.refs_2_, bf16[1024,5504]{1,0:T(8,128)(2,1)} %refs_3_.6, ...), custom_call_target="tpu_custom_call" | custom-call | flops 8800000000 | bytes 240568 | tf_op jit(solution)/shard_map/put_ff/pallas_call | solution.py:46
  332.2 4.9 %put_att.1 = (f32[256,3072]{1,0:T(8,128)}, f32[256,1024]{1,0:T(8,128)}, f32[1,256]{1,0:T(1,128)}) custom-call(s32[78]{0:T(128)} %dynamic-slice_bitcast_fusion.refs_0_, bf16[1,4,32,4096]{3,2,1,0:T(8,128)(2,1)} %join.7.refs_5_.refs_1_, bf16[1,4,32,4096]{3,2,1,0:T(8,128)(2,1)} %collective-permute-done.25.refs_2_, bf16[1024,3072]{1,0:T(8,128)(2,1)} %refs_3_.7, ...), custom_call_target="tpu_custom_call" | custom-call | flops 8800000000 | bytes 125880 | tf_op jit(solution)/shard_map/put_att/pallas_call | solution.py:46
  (20 shorter events, 0.1 us)
Async XLA Ops:
  2.3 18.4 %collective-permute-start = (bf16[2,64,1024]{2,1,0:T(8,128)(2,1)}, bf16[2,64,1024]{2,1,0:T(8,128)(2,1)}, u32[]{:S(2)}, u32[]{:S(2)}) collective-permute-start(bf16[2,64,1024]{2,1,0:T(8,128)(2,1)} %slice.3), channel_id=1, source_target_pairs={{0,1},{1,2},{2,3},{4,5},{5,6},{6,7},{8,9},{9,10},{10,11},{12,13},{... | collective-permute-start | bytes 786440 | tf_op jit(solution)/shard_map/ppermute | solution.py:1007
  73.7 4.4 %collective-permute-start.1 = (bf16[512,1536]{1,0:T(8,128)(2,1)}, bf16[512,1536]{1,0:T(8,128)(2,1)}, u32[]{:S(2)}, u32[]{:S(2)}) collective-permute-start(bf16[512,1536]{1,0:T(8,128)(2,1)} %get-tuple-element.73), channel_id=1, source_target_pairs={{0,4},{1,5},{2,6},{3,7},{4,0},{5,1},{6,2},{7,3},{8,12},{9,13},{10,... | collective-permute-start | bytes 4718600 | tf_op jit(solution)/shard_map/ppermute | solution.py:761
  74.7 5.6 %collective-permute-start.2 = (bf16[512,1536]{1,0:T(8,128)(2,1)}, bf16[512,1536]{1,0:T(8,128)(2,1)}, u32[]{:S(2)}, u32[]{:S(2)}) collective-permute-start(bf16[512,1536]{1,0:T(8,128)(2,1)} %get-tuple-element.74), channel_id=1, source_target_pairs={{0,4},{1,5},{2,6},{3,7},{4,0},{5,1},{6,2},{7,3},{8,12},{9,13},{10,... | collective-permute-start | bytes 4718600 | tf_op jit(solution)/shard_map/ppermute | solution.py:761
  74.8 7.8 %collective-permute-start.3 = (bf16[512,1536]{1,0:T(8,128)(2,1)}, bf16[512,1536]{1,0:T(8,128)(2,1)}, u32[]{:S(2)}, u32[]{:S(2)}) collective-permute-start(bf16[512,1536]{1,0:T(8,128)(2,1)} %get-tuple-element.75), channel_id=1, source_target_pairs={{0,4},{1,5},{2,6},{3,7},{4,0},{5,1},{6,2},{7,3},{8,12},{9,13},{10,... | collective-permute-start | bytes 4718600 | tf_op jit(solution)/shard_map/ppermute | solution.py:761
  94.9 34.5 %collective-permute-start.7 = (bf16[3,256,1536]{2,1,0:T(8,128)(2,1)}, bf16[3,256,1536]{2,1,0:T(8,128)(2,1)}, u32[]{:S(2)}, u32[]{:S(2)}) collective-permute-start(bf16[3,256,1536]{2,1,0:T(8,128)(2,1)} %get-tuple-element.76.refs_13_), channel_id=1, source_target_pairs={{0,16},{1,17},{2,18},{3,19},{4,5},{5,4},{6,7},{7,6},{8,24},{9,25},... | collective-permute-start | bytes 7077896 | tf_op jit(solution)/shard_map/ppermute | solution.py:761
  127.8 6.2 %collective-permute-start.4 = (bf16[512,1280]{1,0:T(8,128)(2,1)}, bf16[512,1280]{1,0:T(8,128)(2,1)}, u32[]{:S(2)}, u32[]{:S(2)}) collective-permute-start(bf16[512,1280]{1,0:T(8,128)(2,1)} %get-tuple-element.84), channel_id=1, source_target_pairs={{0,4},{1,5},{2,6},{3,7},{4,0},{5,1},{6,2},{7,3},{8,12},{9,13},{10,... | collective-permute-start | bytes 3932168 | tf_op jit(solution)/shard_map/ppermute | solution.py:761
  128.9 5.1 %collective-permute-start.5 = (bf16[512,1280]{1,0:T(8,128)(2,1)}, bf16[512,1280]{1,0:T(8,128)(2,1)}, u32[]{:S(2)}, u32[]{:S(2)}) collective-permute-start(bf16[512,1280]{1,0:T(8,128)(2,1)} %get-tuple-element.85), channel_id=1, source_target_pairs={{0,4},{1,5},{2,6},{3,7},{4,0},{5,1},{6,2},{7,3},{8,12},{9,13},{10,... | collective-permute-start | bytes 3932168 | tf_op jit(solution)/shard_map/ppermute | solution.py:761
  129.0 6.7 %collective-permute-start.6 = (bf16[512,1280]{1,0:T(8,128)(2,1)}, bf16[512,1280]{1,0:T(8,128)(2,1)}, u32[]{:S(2)}, u32[]{:S(2)}) collective-permute-start(bf16[512,1280]{1,0:T(8,128)(2,1)} %get-tuple-element.86), channel_id=1, source_target_pairs={{0,4},{1,5},{2,6},{3,7},{4,0},{5,1},{6,2},{7,3},{8,12},{9,13},{10,... | collective-permute-start | bytes 3932168 | tf_op jit(solution)/shard_map/ppermute | solution.py:761
  133.8 30.4 %collective-permute-start.8 = (bf16[3,128,1536]{2,1,0:T(8,128)(2,1)}, bf16[3,128,1536]{2,1,0:T(8,128)(2,1)}, u32[]{:S(2)}, u32[]{:S(2)}) collective-permute-start(bf16[3,128,1536]{2,1,0:T(8,128)(2,1)} %get-tuple-element.88.refs_8_), channel_id=1, source_target_pairs={{0,8},{1,9},{2,10},{3,11},{4,20},{5,21},{6,22},{7,23},{8,0},{9,1},... | collective-permute-start | bytes 3538952 | tf_op jit(solution)/shard_map/ppermute | solution.py:761
  146.9 39.0 %collective-permute-start.10 = (bf16[3,256,1280]{2,1,0:T(8,128)(2,1)}, bf16[3,256,1280]{2,1,0:T(8,128)(2,1)}, u32[]{:S(2)}, u32[]{:S(2)}) collective-permute-start(bf16[3,256,1280]{2,1,0:T(8,128)(2,1)} %get-tuple-element.89.refs_8_), channel_id=1, source_target_pairs={{0,16},{1,17},{2,18},{3,19},{4,5},{5,4},{6,7},{7,6},{8,24},{9,25},... | collective-permute-start | bytes 5898248 | tf_op jit(solution)/shard_map/ppermute | solution.py:761
  185.8 14.9 %collective-permute-start.9 = (bf16[512,4096]{1,0:T(8,128)(2,1)}, bf16[512,4096]{1,0:T(8,128)(2,1)}, u32[]{:S(2)}, u32[]{:S(2)}) collective-permute-start(bf16[512,4096]{1,0:T(8,128)(2,1)} %att_grad.2.refs_5_), channel_id=1, source_target_pairs={{0,4},{1,5},{2,6},{3,7},{4,0},{5,1},{6,2},{7,3},{8,12},{9,13},{10,... | collective-permute-start | bytes 12582920 | tf_op jit(solution)/shard_map/ppermute | solution.py:761
  190.8 21.6 %collective-permute-start.13 = (bf16[3,128,1280]{2,1,0:T(8,128)(2,1)}, bf16[3,128,1280]{2,1,0:T(8,128)(2,1)}, u32[]{:S(2)}, u32[]{:S(2)}) collective-permute-start(bf16[3,128,1280]{2,1,0:T(8,128)(2,1)} %get-tuple-element.99), channel_id=1, source_target_pairs={{0,8},{1,9},{2,10},{3,11},{4,20},{5,21},{6,22},{7,23},{8,0},{9,1},... | collective-permute-start | bytes 2949128 | tf_op jit(solution)/shard_map/ppermute | solution.py:761
  196.7 15.6 %collective-permute-start.12 = (bf16[3,64,1536]{2,1,0:T(8,128)(2,1)}, bf16[3,64,1536]{2,1,0:T(8,128)(2,1)}, u32[]{:S(2)}, u32[]{:S(2)}) collective-permute-start(bf16[3,64,1536]{2,1,0:T(8,128)(2,1)} %get-tuple-element.94.refs_5_), channel_id=1, source_target_pairs={{0,1},{1,0},{2,3},{3,2},{4,12},{5,13},{6,14},{7,15},{8,9},{9,8},{1... | collective-permute-start | bytes 1769480 | tf_op jit(solution)/shard_map/ppermute | solution.py:761
  197.9 14.4 %collective-permute-start.14 = (bf16[128,1024]{1,0:T(8,128)(2,1)}, bf16[128,1024]{1,0:T(8,128)(2,1)}, u32[]{:S(2)}, u32[]{:S(2)}) collective-permute-start(bf16[128,1024]{1,0:T(8,128)(2,1)} %rim_grad.1.refs_8_), channel_id=1, source_target_pairs={{1,0},{2,1},{3,2},{5,4},{6,5},{7,6},{9,8},{10,9},{11,10},{13,12},{... | collective-permute-start | bytes 786440 | tf_op jit(solution)/shard_map/ppermute | solution.py:1007
  212.3 39.5 %collective-permute-start.11 = (bf16[1,256,4096]{2,1,0:T(8,128)(2,1)}, bf16[1,256,4096]{2,1,0:T(8,128)(2,1)}, u32[]{:S(2)}, u32[]{:S(2)}) collective-permute-start(bf16[1,256,4096]{2,1,0:T(8,128)(2,1)} %bitcast.46), channel_id=1, source_target_pairs={{0,16},{1,17},{2,18},{3,19},{4,5},{5,4},{6,7},{7,6},{8,24},{9,25},... | collective-permute-start | bytes 6291464 | tf_op jit(solution)/shard_map/ppermute | solution.py:761
  215.8 36.0 %collective-permute-start.15 = (bf16[3,64,1280]{2,1,0:T(8,128)(2,1)}, bf16[3,64,1280]{2,1,0:T(8,128)(2,1)}, u32[]{:S(2)}, u32[]{:S(2)}) collective-permute-start(bf16[3,64,1280]{2,1,0:T(8,128)(2,1)} %get-tuple-element.101), channel_id=1, source_target_pairs={{0,1},{1,0},{2,3},{3,2},{4,12},{5,13},{6,14},{7,15},{8,9},{9,8},{1... | collective-permute-start | bytes 1474568 | tf_op jit(solution)/shard_map/ppermute | solution.py:761
  216.1 35.8 %collective-permute-start.16 = (bf16[3,32,1536]{2,1,0:T(8,128)(2,1)}, bf16[3,32,1536]{2,1,0:T(8,128)(2,1)}, u32[]{:S(2)}, u32[]{:S(2)}) collective-permute-start(bf16[3,32,1536]{2,1,0:T(8,128)(2,1)} %get-tuple-element.102.refs_6_), channel_id=1, source_target_pairs={{0,2},{1,3},{2,0},{3,1},{4,6},{5,7},{6,4},{7,5},{8,10},{9,11},{10,... | collective-permute-start | bytes 884744 | tf_op jit(solution)/shard_map/ppermute | solution.py:761
  256.2 17.2 %collective-permute-start.17 = (bf16[1,128,4096]{2,1,0:T(8,128)(2,1)}, bf16[1,128,4096]{2,1,0:T(8,128)(2,1)}, u32[]{:S(2)}, u32[]{:S(2)}) collective-permute-start(bf16[1,128,4096]{2,1,0:T(8,128)(2,1)} %get-tuple-element.103.refs_4_), channel_id=1, source_target_pairs={{0,8},{1,9},{2,10},{3,11},{4,20},{5,21},{6,22},{7,23},{8,0},{9,1},... | collective-permute-start | bytes 3145736 | tf_op jit(solution)/shard_map/ppermute | solution.py:761
  256.2 20.2 %collective-permute-start.19 = (bf16[3,32,1280]{2,1,0:T(8,128)(2,1)}, bf16[3,32,1280]{2,1,0:T(8,128)(2,1)}, u32[]{:S(2)}, u32[]{:S(2)}) collective-permute-start(bf16[3,32,1280]{2,1,0:T(8,128)(2,1)} %get-tuple-element.109), channel_id=1, source_target_pairs={{0,2},{1,3},{2,0},{3,1},{4,6},{5,7},{6,4},{7,5},{8,10},{9,11},{10,... | collective-permute-start | bytes 737288 | tf_op jit(solution)/shard_map/ppermute | solution.py:761
  276.4 10.8 %collective-permute-start.18 = (bf16[1,64,4096]{2,1,0:T(8,128)(2,1)}, bf16[1,64,4096]{2,1,0:T(8,128)(2,1)}, u32[]{:S(2)}, u32[]{:S(2)}) collective-permute-start(bf16[1,64,4096]{2,1,0:T(8,128)(2,1)} %get-tuple-element.106.refs_4_), channel_id=1, source_target_pairs={{0,1},{1,0},{2,3},{3,2},{4,12},{5,13},{6,14},{7,15},{8,9},{9,8},{1... | collective-permute-start | bytes 1572872 | tf_op jit(solution)/shard_map/ppermute | solution.py:761
  278.6 20.2 %collective-permute-start.21 = (bf16[3,1,32,2816]{3,2,1,0:T(8,128)(2,1)}, bf16[3,1,32,2816]{3,2,1,0:T(8,128)(2,1)}, u32[]{:S(2)}, u32[]{:S(2)}) collective-permute-start(bf16[3,1,32,2816]{3,2,1,0:T(8,128)(2,1)} %bitcast.47), channel_id=1, source_target_pairs={{0,16},{1,17},{2,18},{3,19},{4,12},{5,13},{6,14},{7,15},{8,24},{9,... | collective-permute-start | bytes 1622024 | tf_op jit(solution)/shard_map/ppermute | solution.py:761
  289.8 11.7 %collective-permute-start.20 = (bf16[1,32,4096]{2,1,0:T(8,128)(2,1)}, bf16[1,32,4096]{2,1,0:T(8,128)(2,1)}, u32[]{:S(2)}, u32[]{:S(2)}) collective-permute-start(bf16[1,32,4096]{2,1,0:T(8,128)(2,1)} %get-tuple-element.111.refs_3_), channel_id=1, source_target_pairs={{0,2},{1,3},{2,0},{3,1},{4,6},{5,7},{6,4},{7,5},{8,10},{9,11},{10,... | collective-permute-start | bytes 786440 | tf_op jit(solution)/shard_map/ppermute | solution.py:761
  301.5 14.3 %collective-permute-start.24 = (bf16[3,2,32,2816]{3,2,1,0:T(8,128)(2,1)}, bf16[3,2,32,2816]{3,2,1,0:T(8,128)(2,1)}, u32[]{:S(2)}, u32[]{:S(2)}) collective-permute-start(bf16[3,2,32,2816]{3,2,1,0:T(8,128)(2,1)} %join.4.refs_2_.refs_1_), channel_id=1, source_target_pairs={{0,8},{1,9},{2,10},{3,11},{4,20},{5,21},{6,22},{7,23},{8,0},{9,1},... | collective-permute-start | bytes 3244040 | tf_op jit(solution)/shard_map/ppermute | solution.py:761
  303.3 7.3 %collective-permute-start.22 = (bf16[1,1,32,4096]{3,2,1,0:T(8,128)(2,1)}, bf16[1,1,32,4096]{3,2,1,0:T(8,128)(2,1)}, u32[]{:S(2)}, u32[]{:S(2)}) collective-permute-start(bf16[1,1,32,4096]{3,2,1,0:T(8,128)(2,1)} %bitcast.50), channel_id=1, source_target_pairs={{0,16},{1,17},{2,18},{3,19},{4,12},{5,13},{6,14},{7,15},{8,24},{9,... | collective-permute-start | bytes 786440 | tf_op jit(solution)/shard_map/ppermute | solution.py:761
  313.1 8.4 %collective-permute-start.23 = (bf16[1,2,32,4096]{3,2,1,0:T(8,128)(2,1)}, bf16[1,2,32,4096]{3,2,1,0:T(8,128)(2,1)}, u32[]{:S(2)}, u32[]{:S(2)}) collective-permute-start(bf16[1,2,32,4096]{3,2,1,0:T(8,128)(2,1)} %join.5.refs_3_.refs_1_), channel_id=1, source_target_pairs={{0,8},{1,9},{2,10},{3,11},{4,20},{5,21},{6,22},{7,23},{8,0},{9,1},... | collective-permute-start | bytes 1572872 | tf_op jit(solution)/shard_map/ppermute | solution.py:761
  319.1 5.0 %collective-permute-start.26 = (bf16[3,4,32,2816]{3,2,1,0:T(8,128)(2,1)}, bf16[3,4,32,2816]{3,2,1,0:T(8,128)(2,1)}, u32[]{:S(2)}, u32[]{:S(2)}) collective-permute-start(bf16[3,4,32,2816]{3,2,1,0:T(8,128)(2,1)} %join.6.refs_3_.refs_1_), channel_id=1, source_target_pairs={{0,4},{1,5},{2,6},{3,7},{4,0},{5,1},{6,2},{7,3},{8,12},{9,13},{10,... | collective-permute-start | bytes 6488072 | tf_op jit(solution)/shard_map/ppermute | solution.py:761
  324.2 8.0 %collective-permute-start.25 = (bf16[1,4,32,4096]{3,2,1,0:T(8,128)(2,1)}, bf16[1,4,32,4096]{3,2,1,0:T(8,128)(2,1)}, u32[]{:S(2)}, u32[]{:S(2)}) collective-permute-start(bf16[1,4,32,4096]{3,2,1,0:T(8,128)(2,1)} %join.7.refs_5_.refs_1_), channel_id=1, source_target_pairs={{0,4},{1,5},{2,6},{3,7},{4,0},{5,1},{6,2},{7,3},{8,12},{9,13},{10,... | collective-permute-start | bytes 3145736 | tf_op jit(solution)/shard_map/ppermute | solution.py:761
